TPU v7x, 256 devices: a whole 4x4x8 slice. The times are simulated.
256 devices in a mesh: head: 8 (over x, core), expert: 32 (over z, y).
Axes of the slice: x: 4, y: 4, z: 8, core: 2. Of those that a mesh axis runs over, the one named last changes fastest.
Arguments:
- queries: bfloat16 [512, 128, 576], P('expert', 'head'), may hold values from -64 to 64
- resident_cache: bfloat16 [128, 256, 576], P('expert'), may hold values from -6 to 6
- resident_len: int32 [128], P('expert'), may hold values from 1 to 256, as said below
- new_cache: bfloat16 [384, 64, 576], P('expert'), may hold values from -6 to 6
- new_len: int32 [384], replicated, may hold values from 1 to 64, as said below
- new_owner: int32 [384], replicated, may hold values from 0 to 31, as said below
- value_up: bfloat16 [128, 512, 128], P('head'), may hold values from -0.25 to 0.25
- w_output: bfloat16 [16384, 7168], P('head', 'expert'), may hold values from -0.046875 to 0.046875
- residual: bfloat16 [512, 7168], P(None, 'expert'), may hold values from -6 to 6
- expert_ids: int32 [512, 8], replicated, may hold values from 0 to 31, all different within a row; in each aligned block of 16 rows (0 to 15, 16 to 31, ...) at most 6 rows name the same one
- expert_gates: float32 [512, 8], replicated, may hold values from 0.1 to 1
- norm_gain: bfloat16 [7168], replicated, may hold values from 0.5 to 1.5
- w_gate: bfloat16 [32, 7168, 1024], P('expert', None, 'head'), may hold values from -0.0625 to 0.0625
- w_up: bfloat16 [32, 7168, 1024], P('expert', None, 'head'), may hold values from -0.0625 to 0.0625
- w_down: bfloat16 [32, 1024, 7168], P('expert', 'head'), may hold values from -0.1875 to 0.1875
Outputs:
- layer_out: bfloat16 [512, 7168], P('head', 'expert')
Inputs may be any that keep to these rules, and one draw needn't show every extreme that they name: `resident_len`: every decode owner has a resident request of length 256. `new_len`: every prefill device holds a new request of length 64. `new_owner`: one prefill device sends at most 2 of its 12 new requests to one decode owner, and every decode owner receives exactly 12 in all; a prefill device sends either 2 or none to each owner, except to at most one owner, which gets the remainder of 12 divided by 2. `expert_ids`: in each aligned block of 16 rows (the rows of one decode owner) no expert is named by more than 6 rows; the 8 experts of a row differ.
All inputs are finite; a program needn't handle non-finite values.
Results may differ from a plain program's by a relative error of at most 0.012.
Values may be sent and summed in bfloat16 or wider, within the bound.
No kernel may reach another device: no remote copies, remote signals or barrier semaphores. Data moves between devices by JAX's collectives and lax.ppermute only.
A program may use at most 128 MiB of HBM per device.

v0:
```python
import functools

import jax
import jax.numpy as jnp
from jax import lax
from jax.experimental import pallas as pl
from jax.experimental.pallas import tpu as pltpu
from jax.sharding import Mesh
from jax.sharding import PartitionSpec as P

ROPE = 64
NOPE = 128
EXPERT = ("expert_0", "expert_1")
HEAD = ("head_0", "head_1")
MOST = 2
CAP = 6
BF = jnp.bfloat16
F32 = jnp.float32
I32 = jnp.int32
VMEM_BYTES = 48 * 1024 * 1024


def params():
    return pltpu.CompilerParams(vmem_limit_bytes=VMEM_BYTES)


def whole(memory=pltpu.VMEM):
    return pl.BlockSpec(memory_space=memory)


def shifted(x, axis, step):
    n = lax.axis_size(axis)
    return lax.ppermute(x, axis, [(i, (i + step) % n) for i in range(n)])


def ring_gather(x, axis):
    n = lax.axis_size(axis)
    far = n // 2
    cut = x.shape[0] // 2
    found = {0: x}
    right, left = x, x
    for step in range(1, far):
        right, left = shifted(right, axis, 1), shifted(left, axis, -1)
        found[step], found[n - step] = right, left
    found[far] = (shifted(right[:cut], axis, 1), shifted(left[cut:], axis, -1))
    return [found[d] for d in range(n)]


def flat(pieces):
    out = []
    for piece in pieces:
        out.extend(piece if isinstance(piece, tuple) else (piece,))
    return out


def attend(queries, caches_t, length, value_up):
    inverse_root = (NOPE + ROPE) ** (-0.5)
    latent_width = value_up.shape[1]
    scores = jnp.einsum("rhc,rct->rht", queries, caches_t, preferred_element_type=F32) * inverse_root
    inside = lax.broadcasted_iota(I32, scores.shape, 2) < length[:, None, None]
    scores = jnp.where(inside, scores, -jnp.inf)
    highest = jnp.max(scores, axis=2, keepdims=True)
    raised = jnp.exp(scores - highest)
    weights = (raised / jnp.sum(raised, axis=2, keepdims=True)).astype(BF)
    latent = jnp.einsum("rht,rct->rhc", weights, caches_t[:, :latent_width], preferred_element_type=F32).astype(BF)
    values = jnp.einsum("rhc,hcv->rhv", latent, value_up, preferred_element_type=F32).astype(BF)
    return values.reshape(values.shape[0], -1)


def pack_kernel(owners, turns, at, cache_ref, out_ref, sems):
    span = out_ref.shape[1]
    first = pl.multiple_of(at[0] * span, span)

    def copy(i):
        return pltpu.make_async_copy(
            cache_ref.at[i, pl.ds(first, span)], out_ref.at[owners[i]], sems.at[i]
        )

    for i in range(cache_ref.shape[0]):

        @pl.when(turns[i] == at[1])
        def _():
            copy(i).start()

    for i in range(cache_ref.shape[0]):

        @pl.when(turns[i] == at[1])
        def _():
            copy(i).wait()


def pack_cache(owners, turns, at, cache, span, n_expert):
    return pl.pallas_call(
        pack_kernel,
        out_shape=jax.ShapeDtypeStruct((n_expert, span, cache.shape[2]), cache.dtype),
        in_specs=[whole(pltpu.SMEM)] * 3 + [whole(pl.ANY)],
        out_specs=whole(pl.ANY),
        scratch_shapes=[pltpu.SemaphoreType.DMA((cache.shape[0],))],
        compiler_params=params(),
        name="pack_cache",
    )(owners, turns, at, cache)


def select_kernel(sources, arrived_ref, out_ref, sems):
    copies = [
        pltpu.make_async_copy(arrived_ref.at[sources[k]], out_ref.at[k], sems.at[k])
        for k in range(out_ref.shape[0])
    ]
    for copy in copies:
        copy.start()
    for copy in copies:
        copy.wait()


def select_arrived(sources, arrived):
    count = sources.shape[0]
    return pl.pallas_call(
        select_kernel,
        out_shape=jax.ShapeDtypeStruct((count,) + arrived.shape[1:], arrived.dtype),
        in_specs=[whole(pltpu.SMEM), whole(pl.ANY)],
        out_specs=whole(pl.ANY),
        scratch_shapes=[pltpu.SemaphoreType.DMA((count,))],
        compiler_params=params(),
        name="select_arrived",
    )(sources, arrived)


def new_attention_kernel(lens, at, q_ref, up_ref, res_ref, *refs):
    pieces, out_ref, latents = refs[:-2], refs[-2], refs[-1]
    ring = len(pieces) // 2
    pairs, span = pieces[0].shape[0], pieces[0].shape[1]
    old = res_ref.shape[0]
    count = pairs * MOST
    heads, latent_width, value_width = up_ref.shape
    inverse_root = (NOPE + ROPE) ** (-0.5)
    place, core = at[0], at[1]
    column = lax.broadcasted_iota(I32, (heads, ring * span), 1)
    position = ((place + ring - column // span) % ring) * span + column % span
    for i in range(count):
        k, turn = i // MOST, i % MOST
        ours = core == turn
        cache = jnp.concatenate(
            [jnp.where(ours, pieces[d][k], pieces[ring + d][k]) for d in range(ring)], axis=0
        )
        scores = (
            lax.dot_general(q_ref[old + i], cache, (((1,), (1,)), ((), ())), preferred_element_type=F32)
            * inverse_root
        )
        scores = jnp.where(position < lens[i], scores, -jnp.inf)
        raised = jnp.exp(scores - jnp.max(scores, axis=1, keepdims=True))
        weights = (raised / jnp.sum(raised, axis=1, keepdims=True)).astype(BF)
        latents[:, i, :] = jnp.dot(weights, cache[:, :latent_width], preferred_element_type=F32)
    for h in range(heads):
        values = jnp.dot(latents[h, :, :].astype(BF), up_ref[h], preferred_element_type=F32)
        rows = jnp.concatenate(
            [res_ref[:, h * value_width : (h + 1) * value_width].astype(F32), values[:count]], axis=0
        ).astype(BF)
        out_ref[:, h * value_width : (h + 1) * value_width] = rows


def new_attention(lens, at, queries, value_up, resident, pieces):
    heads, latent_width, value_width = value_up.shape
    rows = queries.shape[0]
    return pl.pallas_call(
        new_attention_kernel,
        out_shape=jax.ShapeDtypeStruct((rows, heads * value_width), BF),
        in_specs=[whole(pltpu.SMEM)] * 2 + [whole()] * (3 + len(pieces)),
        out_specs=whole(),
        scratch_shapes=[pltpu.VMEM((heads, rows, latent_width), F32)],
        compiler_params=params(),
        name="new_attention",
    )(lens, at, queries, value_up, resident, *pieces)


def plan_kernel(rows_dev, ids_ref, gates_ref, sel_ref, mix_ref):
    rows, choose = ids_ref.shape
    slots_all = sel_ref.shape[1]
    slots = rows // rows_dev * CAP
    experts = slots_all // slots
    expert = lax.broadcasted_iota(I32, (rows, experts), 1)
    member = jnp.zeros((rows, experts), F32)
    gate = jnp.zeros((rows, experts), F32)
    for k in range(choose):
        same = ids_ref[:, k : k + 1] == expert
        member = jnp.where(same, 1.0, member)
        gate = jnp.where(same, gates_ref[:, k : k + 1], gate)
    to_row = lax.broadcasted_iota(I32, (rows, rows), 0)
    from_row = lax.broadcasted_iota(I32, (rows, rows), 1)
    before = (from_row < to_row) & (from_row // rows_dev == to_row // rows_dev)
    rank = jnp.dot(before.astype(F32).astype(BF), member.astype(BF), preferred_element_type=F32)
    block = lax.broadcasted_iota(I32, (rows, experts), 0) // rows_dev
    slot = jnp.where(member > 0, rank + (block * CAP).astype(F32), -1.0)
    spread = (
        lax.broadcasted_iota(I32, (experts, slots_all), 0)
        == lax.broadcasted_iota(I32, (experts, slots_all), 1) // slots
    ).astype(F32)
    slot_wide = jnp.dot(slot.astype(BF), spread.astype(BF), preferred_element_type=F32)
    gate_wide = jnp.dot(gate, spread, preferred_element_type=F32, precision=lax.Precision.HIGHEST)
    wanted = (lax.broadcasted_iota(I32, (rows, slots_all), 1) % slots).astype(F32)
    hit = slot_wide == wanted
    sel_ref[...] = jnp.where(hit, 1.0, 0.0).astype(BF)
    mix_ref[...] = jnp.where(hit, gate_wide, 0.0)


def plan(ids, gates, rows_dev, experts):
    rows = ids.shape[0]
    slots_all = experts * (rows // rows_dev) * CAP
    return pl.pallas_call(
        functools.partial(plan_kernel, rows_dev),
        out_shape=(
            jax.ShapeDtypeStruct((rows, slots_all), BF),
            jax.ShapeDtypeStruct((rows, slots_all), F32),
        ),
        in_specs=[whole()] * 2,
        out_specs=(whole(), whole()),
        compiler_params=params(),
        name="plan",
    )(ids, gates)


def dispatch_kernel(parts_ref, residual_ref, sel_ref, hidden_ref, out_ref):
    total = parts_ref[0].astype(F32)
    for k in range(1, parts_ref.shape[0]):
        total = total + parts_ref[k].astype(F32)
    hidden = (residual_ref[...].astype(F32) + total).astype(BF)
    hidden_ref[...] = hidden
    picked = lax.dot_general(sel_ref[...], hidden, (((0,), (0,)), ((), ())), preferred_element_type=F32)
    out_ref[...] = picked.reshape(out_ref.shape).astype(BF)


def dispatch(parts, residual, sel, experts):
    rows, columns = residual.shape
    return pl.pallas_call(
        dispatch_kernel,
        out_shape=(
            jax.ShapeDtypeStruct((rows, columns), BF),
            jax.ShapeDtypeStruct((experts, sel.shape[1] // experts, columns), BF),
        ),
        in_specs=[whole()] * 3,
        out_specs=(whole(), whole()),
        compiler_params=params(),
        name="dispatch",
    )(parts, residual, sel)


def norm_kernel(x_ref, gain_ref, out_ref):
    x = x_ref[...].astype(F32)
    width = x.shape[0] * x.shape[2]
    squares = jnp.sum(jnp.sum(x * x, axis=0), axis=1, keepdims=True)
    inverse = lax.rsqrt(squares / width + 1e-06)
    out_ref[...] = (x * inverse[None] * gain_ref[...].astype(F32)).astype(BF)


def normed_rows(x, gain):
    return pl.pallas_call(
        norm_kernel,
        out_shape=jax.ShapeDtypeStruct(x.shape, BF),
        in_specs=[whole()] * 2,
        out_specs=whole(),
        compiler_params=params(),
        name="norm",
    )(x, gain)


def experts_kernel(layout, *refs):
    count = sum(layout)
    x_refs, (gate_ref, up_ref, down_ref), outs = refs[:count], refs[count : count + 3], refs[count + 3 :]
    columns, slots = x_refs[0].shape[0], x_refs[0].shape[1]
    width = x_refs[0].shape[2]
    gate = up = None
    for j in range(columns):
        pieces, at = [], 0
        for parts in layout:
            split = columns // parts
            pieces.append(x_refs[at + j // split][j % split].astype(F32))
            at += parts
        x = jnp.concatenate(pieces, axis=0).astype(BF)
        g = jnp.dot(x, gate_ref[j], preferred_element_type=F32)
        u = jnp.dot(x, up_ref[j], preferred_element_type=F32)
        gate, up = (g, u) if gate is None else (gate + g, up + u)
    act = (gate * jax.nn.sigmoid(gate) * up).astype(BF)
    for j in range(columns):
        y = jnp.dot(act, down_ref[:, j * width : (j + 1) * width], preferred_element_type=F32)
        for k, out in enumerate(outs):
            out[j] = y[k * slots : (k + 1) * slots].astype(out.dtype)


def run_experts(layout, pieces, w_gate, w_up, w_down, types):
    shape = pieces[0].shape
    return pl.pallas_call(
        functools.partial(experts_kernel, layout),
        out_shape=tuple(jax.ShapeDtypeStruct(shape, kind) for kind in types),
        in_specs=[whole()] * (len(pieces) + 3),
        out_specs=tuple(whole() for _ in types),
        compiler_params=params(),
        name="experts",
    )(*pieces, w_gate, w_up, w_down)


def combine_kernel(back_ref, mix_ref, hidden_ref, out_ref):
    back = back_ref[...].astype(F32).reshape(-1, back_ref.shape[2])
    routed = jnp.dot(mix_ref[...], back, preferred_element_type=F32, precision=lax.Precision.HIGHEST)
    out_ref[...] = (hidden_ref[...].astype(F32) + routed).astype(BF)


def combine(back, mix, hidden):
    return pl.pallas_call(
        combine_kernel,
        out_shape=jax.ShapeDtypeStruct(hidden.shape, BF),
        in_specs=[whole()] * 3,
        out_specs=whole(),
        compiler_params=params(),
        name="combine",
    )(back, mix, hidden)


def exchange(x, axes):
    return lax.all_to_all(x, axes, split_axis=0, concat_axis=0, tiled=True)


def gather_over_head(x):
    near = ring_gather(x, HEAD[0])
    layout = [len(p) if isinstance(p, tuple) else 1 for p in near]
    near = flat(near)
    far = [shifted(p, HEAD[1], 1) for p in near]
    return layout * 2, near + far


def sum_over_head(kept, sent):
    other = [shifted(s, HEAD[1], 1) for s in (sent[2], sent[1], sent[3], sent[0])]
    other = [other[3], other[1], other[0], other[2]]
    pair = [k + o.astype(F32) for k, o in zip(kept, other)]
    cut = pair[2].shape[0] // 2
    far = pair[2].astype(BF)
    low = shifted(far[:cut], HEAD[0], -1).astype(F32)
    high = shifted(far[cut:], HEAD[0], 1).astype(F32)
    before = jnp.concatenate([pair[1][:cut] + low, pair[1][cut:]], axis=0).astype(BF)
    after = jnp.concatenate([pair[3][:cut], pair[3][cut:] + high], axis=0).astype(BF)
    from_after = shifted(before, HEAD[0], -1).astype(F32)
    from_before = shifted(after, HEAD[0], 1).astype(F32)
    return (pair[0] + from_after + from_before).astype(BF)


def per_device(
    queries,
    resident_cache,
    resident_len,
    new_cache,
    new_len,
    new_owner,
    value_up,
    w_output,
    residual,
    expert_ids,
    expert_gates,
    norm_gain,
    w_gate,
    w_up,
    w_down,
):
    n_expert = lax.axis_size(EXPERT)
    n_head = lax.axis_size(HEAD)
    me = lax.axis_index(EXPERT)
    head = lax.axis_index(HEAD)
    req_count = resident_cache.shape[0]
    new_count = new_cache.shape[0]
    rows_dev = req_count + new_count
    rows_all = rows_dev * n_expert
    block_rows = rows_all // n_head
    columns = residual.shape[1]
    news = new_owner.shape[0]

    x, core = lax.axis_index(HEAD[0]), lax.axis_index(HEAD[1])
    ring = lax.axis_size(HEAD[0])
    number = jnp.arange(news, dtype=I32)
    equal = (new_owner[:, None] == new_owner[None, :]) & (number[None, :] < number[:, None])
    place = jnp.sum(equal.astype(I32), axis=1)
    owners = lax.dynamic_slice_in_dim(new_owner, me * new_count, new_count)
    mine = jnp.arange(new_count, dtype=I32)
    turns = jnp.sum(((owners[:, None] == owners[None, :]) & (mine[None, :] < mine[:, None])).astype(I32), axis=1)
    taken = (new_owner == me)[None, :] & (place[None, :] == mine[:, None])
    sources = jnp.sum(jnp.where(taken, (number // new_count)[None, :], 0), axis=1)[::MOST]
    lens = jnp.sum(jnp.where(taken, new_len[None, :], 0), axis=1)
    at = jnp.stack([x, core]).astype(I32)

    packed = pack_cache(owners, turns, at, new_cache, new_cache.shape[1] // ring, n_expert)
    ours = select_arrived(sources, exchange(packed, EXPERT))
    near = [ours] + [shifted(ours, HEAD[0], d) for d in range(1, ring)]
    pieces = near + [shifted(p, HEAD[1], 1) for p in near]
    resident = attend(queries[:req_count], jnp.swapaxes(resident_cache, 1, 2), resident_len, value_up)
    attention = new_attention(lens, at, queries, value_up, resident, pieces)

    everywhere = exchange(jnp.broadcast_to(attention[None], (n_expert,) + attention.shape), EXPERT)
    mixed = jnp.dot(everywhere.reshape(rows_all, -1), w_output, preferred_element_type=F32).astype(BF)
    parts = exchange(mixed.reshape(n_head, block_rows, columns), HEAD)

    block = lambda a: lax.dynamic_slice_in_dim(a, head * block_rows, block_rows)
    sel, mix = plan(block(expert_ids), block(expert_gates), rows_dev, n_expert)
    hidden, outgoing = dispatch(parts, block(residual), sel, n_expert)
    received = exchange(outgoing, EXPERT)
    normed = normed_rows(received, norm_gain.reshape(n_expert, 1, columns))
    layout, pieces = gather_over_head(normed)
    x_count = lax.axis_size(HEAD[0])
    made = run_experts(
        tuple(layout),
        pieces,
        w_gate.reshape(n_expert, columns, -1),
        w_up.reshape(n_expert, columns, -1),
        w_down.reshape(w_down.shape[1:]),
        [F32] * x_count + [BF] * x_count,
    )
    summed = sum_over_head(made[:x_count], made[x_count:])
    back = exchange(summed, EXPERT)
    return combine(back, mix, hidden)


def solution(mesh):
    finer = Mesh(mesh.devices.reshape(4, 2, 8, 4), ("head_0", "head_1", "expert_0", "expert_1"))
    in_specs = (
        P(EXPERT, HEAD, None),
        P(EXPERT, None, None),
        P(EXPERT),
        P(EXPERT, None, None),
        P(),
        P(),
        P(HEAD, None, None),
        P(HEAD, EXPERT),
        P(None, EXPERT),
        P(),
        P(),
        P(),
        P(EXPERT, None, HEAD),
        P(EXPERT, None, HEAD),
        P(EXPERT, HEAD, None),
    )
    out_specs = P(HEAD, EXPERT)
    return jax.shard_map(
        per_device, mesh=finer, in_specs=in_specs, out_specs=out_specs, check_vma=False
    )
```

profile of v0, /device:TPU:32, one launch (start us, length us, event | category | flops | bytes accessed | tf_op | source)
XLA Modules:
  0.0 215.9 jit_solution(10340320823130584804)
XLA Ops:
  3.7 11.4 %all-to-all-start = ((bf16[32,16,576]{2,1,0:T(8,128)(2,1)}), bf16[32,16,576]{2,1,0:T(8,128)(2,1)}, u32[]{:S(2)}, u32[]{:S(2)}) async-start(bf16[32,16,576]{2,1,0:T(8,128)(2,1)} %pack_cache.1), calls=%async_computation | async-start | bytes 1310720 | tf_op jit(solution)/shard_map/all_to_all | solution.py:318
  15.6 1.7 fusion.2
  17.4 17.5 %all-to-all-done.arrived_ref = bf16[32,16,576]{2,1,0:T(8,128)(2,1)} async-done(((bf16[32,16,576]{2,1,0:T(8,128)(2,1)}), bf16[32,16,576]{2,1,0:T(8,128)(2,1)}, u32[]{:S(2)}, u32[]{:S(2)}) %all-to-all-start) | async-done | bytes 589856 | tf_op jit(solution)/shard_map/all_to_all | solution.py:318
  36.4 2.8 %collective-permute-start.2 = (bf16[6,16,576]{2,1,0:T(8,128)(2,1)S(1)}, bf16[6,16,576]{2,1,0:T(8,128)(2,1)}, u32[]{:S(2)}, u32[]{:S(2)}) collective-permute-start(bf16[6,16,576]{2,1,0:T(8,128)(2,1)S(1)} %select_arrived.1.refs_0_), channel_id=1, source_target_pairs={{0,192},{64,0},{128,64},{192,128},{1,193},{65,1},{129,65},{193,129... | collective-permute-start | bytes 331784 | tf_op jit(solution)/shard_map/ppermute | solution.py:33
  40.9 2.3 %convolution_convert_fusion.1 = bf16[4,16,512]{2,1,0:T(8,128)(2,1)} fusion(bf16[4,576,256]{2,1,0:T(8,128)(2,1)} %bitcast.23, f32[4,16]{1,0:T(4,128)S(1)} %fusion.18, f32[4,16,256]{2,1,0:T(8,128)S(1)} %fusion.2), kind=kOutput, calls=%fused_computation.3 | convolution fusion | flops 16859456 | bytes 1247232 | tf_op jit(solution)/shard_map/rht,rct->rhc/dot_general | solution.py:65
  43.7 2.1 collective-permute-done.1.refs_2_
  48.5 5.7 %new_attention.1 = bf16[16,2048]{1,0:T(8,128)(2,1)S(1)} custom-call(s32[12]{0:T(128)S(1)} %get-tuple-element.30.lens, s32[2]{0:T(128)S(1)} %pad_add_fusion.at, bf16[16,16,576]{2,1,0:T(8,128)(2,1)S(1)} %copy-done.3, bf16[16,512,128]{2,1,0:T(8,128)(2,1)S(1)} %copy-done.1, bf16[4,2048]{1,0:T(4,128)(2,1)S(1)} %fusion.4.res_ref, ...), custom_call_target="tpu_custom_call" | custom-call | tf_op jit(solution)/shard_map/new_attention/pallas_call | solution.py:164
  54.2 1.6 broadcast_in_dim.28
  55.8 5.7 %all-to-all-start.1 = ((bf16[32,16,2048]{2,1,0:T(8,128)(2,1)}), bf16[32,16,2048]{2,1,0:T(8,128)(2,1)S(1)}, u32[]{:S(2)}, u32[]{:S(2)}) async-start(bf16[32,16,2048]{2,1,0:T(8,128)(2,1)} %broadcast_in_dim.28), calls=%async_computation.1 | async-start | bytes 4194304 | tf_op jit(solution)/shard_map/all_to_all | solution.py:318
  62.3 49.2 %all-to-all-done.1 = bf16[32,16,2048]{2,1,0:T(8,128)(2,1)S(1)} async-done(((bf16[32,16,2048]{2,1,0:T(8,128)(2,1)}), bf16[32,16,2048]{2,1,0:T(8,128)(2,1)S(1)}, u32[]{:S(2)}, u32[]{:S(2)}) %all-to-all-start.1) | async-done | bytes 2097184 | tf_op jit(solution)/shard_map/all_to_all | solution.py:318
  113.2 3.4 %all-to-all-start.2 = ((bf16[8,64,224]{2,1,0:T(8,128)(2,1)}), bf16[8,64,224]{2,1,0:T(8,128)(2,1)S(1)}, u32[]{:S(2)}, u32[]{:S(2)}) async-start(bf16[8,64,224]{2,1,0:T(8,128)(2,1)} %bitcast.6), calls=%async_computation.2 | async-start | bytes 524288 | tf_op jit(solution)/shard_map/all_to_all | solution.py:318
  119.1 5.0 %all-to-all-done.2.parts_ref = bf16[8,64,224]{2,1,0:T(8,128)(2,1)S(1)} async-done(((bf16[8,64,224]{2,1,0:T(8,128)(2,1)}), bf16[8,64,224]{2,1,0:T(8,128)(2,1)S(1)}, u32[]{:S(2)}, u32[]{:S(2)}) %all-to-all-start.2) | async-done | bytes 229408 | tf_op jit(solution)/shard_map/all_to_all | solution.py:318
  125.1 5.9 %all-to-all-start.3 = ((bf16[32,24,224]{2,1,0:T(8,128)(2,1)}), bf16[32,24,224]{2,1,0:T(8,128)(2,1)S(1)}, u32[]{:S(2)}, u32[]{:S(2)}) async-start(bf16[32,24,224]{2,1,0:T(8,128)(2,1)} %get-tuple-element.18), calls=%async_computation.3 | async-start | bytes 786432 | tf_op jit(solution)/shard_map/all_to_all | solution.py:318
  131.1 14.2 %all-to-all-done.3.x_ref = bf16[32,24,224]{2,1,0:T(8,128)(2,1)S(1)} async-done(((bf16[32,24,224]{2,1,0:T(8,128)(2,1)}), bf16[32,24,224]{2,1,0:T(8,128)(2,1)S(1)}, u32[]{:S(2)}, u32[]{:S(2)}) %all-to-all-start.3) | async-done | bytes 344096 | tf_op jit(solution)/shard_map/all_to_all | solution.py:318
  147.7 7.4 %collective-permute-done.9.refs_4_ = bf16[32,24,224]{2,1,0:T(8,128)(2,1)S(1)} collective-permute-done((bf16[32,24,224]{2,1,0:T(8,128)(2,1)S(1)}, bf16[32,24,224]{2,1,0:T(8,128)(2,1)S(1)}, u32[]{:S(2)}, u32[]{:S(2)}) %collective-permute-start.9) | collective-permute-done | bytes 344096 | tf_op jit(solution)/shard_map/ppermute | solution.py:33
  157.9 3.0 %collective-permute-done.10.refs_3_ = bf16[16,24,224]{2,1,0:T(8,128)(2,1)S(1)} collective-permute-done((bf16[16,24,224]{2,1,0:T(8,128)(2,1)S(1)}, bf16[16,24,224]{2,1,0:T(8,128)(2,1)S(1)}, u32[]{:S(2)}, u32[]{:S(2)}) %collective-permute-start.10) | collective-permute-done | bytes 172064 | tf_op jit(solution)/shard_map/ppermute | solution.py:33
  160.9 2.5 %collective-permute-done.8.refs_2_ = bf16[16,24,224]{2,1,0:T(8,128)(2,1)S(1)} collective-permute-done((bf16[16,24,224]{2,1,0:T(8,128)(2,1)S(1)}, bf16[16,24,224]{2,1,0:T(8,128)(2,1)S(1)}, u32[]{:S(2)}, u32[]{:S(2)}) %collective-permute-start.8) | collective-permute-done | bytes 172064 | tf_op jit(solution)/shard_map/ppermute | solution.py:33
  164.8 6.7 %experts.1 = (f32[32,24,224]{2,1,0:T(8,128)S(1)}, f32[32,24,224]{2,1,0:T(8,128)}, f32[32,24,224]{2,1,0:T(8,128)}, f32[32,24,224]{2,1,0:T(8,128)}, bf16[32,24,224...) custom-call(bf16[32,24,224]{2,1,0:T(8,128)(2,1)S(1)} %norm.1.refs_0_, ...), custom_call_target="tpu_custom_call" | custom-call | tf_op jit(solution)/shard_map/experts/pallas_call | solution.py:290
  175.0 1.9 collective-permute-start.22
  177.0 4.8 %collective-permute-done.19 = bf16[16,24,224]{2,1,0:T(8,128)(2,1)S(1)} collective-permute-done((bf16[16,24,224]{2,1,0:T(8,128)(2,1)S(1)}, bf16[16,24,224]{2,1,0:T(8,128)(2,1)S(1)}, u32[]{:S(2)}, u32[]{:S(2)}) %collective-permute-start.19) | collective-permute-done | bytes 172064 | tf_op jit(solution)/shard_map/ppermute | solution.py:33
  181.9 1.6 collective-permute-start.20
  184.2 8.1 %collective-permute-done.20 = bf16[32,24,224]{2,1,0:T(8,128)(2,1)S(1)} collective-permute-done((bf16[32,24,224]{2,1,0:T(8,128)(2,1)S(1)}, bf16[32,24,224]{2,1,0:T(8,128)(2,1)S(1)}, u32[]{:S(2)}, u32[]{:S(2)}) %collective-permute-start.20) | collective-permute-done | bytes 344096 | tf_op jit(solution)/shard_map/ppermute | solution.py:33
  192.3 2.8 %collective-permute-done.23 = bf16[32,24,224]{2,1,0:T(8,128)(2,1)S(1)} collective-permute-done((bf16[32,24,224]{2,1,0:T(8,128)(2,1)S(1)}, bf16[32,24,224]{2,1,0:T(8,128)(2,1)S(1)}, u32[]{:S(2)}, u32[]{:S(2)}) %collective-permute-start.23) | collective-permute-done | bytes 344096 | tf_op jit(solution)/shard_map/ppermute | solution.py:33
  195.2 19.5 %all_to_all.25.back_ref = bf16[32,24,224]{2,1,0:T(8,128)(2,1)S(1)} all-to-all(bf16[32,24,224]{2,1,0:T(8,128)(2,1)S(1)} %add_convert_fusion), channel_id=1, replica_groups=mesh['head_0'=4,'head_1'=2,'expert_0'=8,'expert_1'=4] {'expert_0','exper..., dimensions={0} | all-to-all | bytes 688128 | tf_op jit(solution)/shard_map/all_to_all | solution.py:318
  (96 shorter events, 29.0 us)
Async XLA Ops:
  3.7 31.3 %all-to-all-start = ((bf16[32,16,576]{2,1,0:T(8,128)(2,1)}), bf16[32,16,576]{2,1,0:T(8,128)(2,1)}, u32[]{:S(2)}, u32[]{:S(2)}) async-start(bf16[32,16,576]{2,1,0:T(8,128)(2,1)} %pack_cache.1), calls=%async_computation | async-start | bytes 1310720 | tf_op jit(solution)/shard_map/all_to_all | solution.py:318
  36.4 6.8 %collective-permute-start.2 = (bf16[6,16,576]{2,1,0:T(8,128)(2,1)S(1)}, bf16[6,16,576]{2,1,0:T(8,128)(2,1)}, u32[]{:S(2)}, u32[]{:S(2)}) collective-permute-start(bf16[6,16,576]{2,1,0:T(8,128)(2,1)S(1)} %select_arrived.1.refs_0_), channel_id=1, source_target_pairs={{0,192},{64,0},{128,64},{192,128},{1,193},{65,1},{129,65},{193,129... | collective-permute-start | bytes 331784 | tf_op jit(solution)/shard_map/ppermute | solution.py:33
  39.2 6.6 %collective-permute-start.1 = (bf16[6,16,576]{2,1,0:T(8,128)(2,1)S(1)}, bf16[6,16,576]{2,1,0:T(8,128)(2,1)}, u32[]{:S(2)}, u32[]{:S(2)}) collective-permute-start(bf16[6,16,576]{2,1,0:T(8,128)(2,1)S(1)} %select_arrived.1.refs_0_), channel_id=1, source_target_pairs={{0,128},{64,192},{128,0},{192,64},{1,129},{65,193},{129,1},{193,65... | collective-permute-start | bytes 331784 | tf_op jit(solution)/shard_map/ppermute | solution.py:33
  40.0 7.0 %collective-permute-start = (bf16[6,16,576]{2,1,0:T(8,128)(2,1)S(1)}, bf16[6,16,576]{2,1,0:T(8,128)(2,1)}, u32[]{:S(2)}, u32[]{:S(2)}) collective-permute-start(bf16[6,16,576]{2,1,0:T(8,128)(2,1)S(1)} %select_arrived.1.refs_0_), channel_id=1, source_target_pairs={{0,64},{64,128},{128,192},{192,0},{1,65},{65,129},{129,193},{193,1... | collective-permute-start | bytes 331784 | tf_op jit(solution)/shard_map/ppermute | solution.py:33
  43.1 5.1 %collective-permute-start.3 = (bf16[6,16,576]{2,1,0:T(8,128)(2,1)S(1)}, bf16[6,16,576]{2,1,0:T(8,128)(2,1)S(1)}, u32[]{:S(2)}, u32[]{:S(2)}) collective-permute-start(bf16[6,16,576]{2,1,0:T(8,128)(2,1)S(1)} %select_arrived.1.refs_0_), channel_id=1, source_target_pairs={{0,32},{32,0},{1,33},{33,1},{2,34},{34,2},{3,35},{35,3},{4,36},{36... | collective-permute-start | bytes 331784 | tf_op jit(solution)/shard_map/ppermute | solution.py:33
  43.2 5.1 %collective-permute-start.6 = (bf16[6,16,576]{2,1,0:T(8,128)(2,1)}, bf16[6,16,576]{2,1,0:T(8,128)(2,1)S(1)}, u32[]{:S(2)}, u32[]{:S(2)}) collective-permute-start(bf16[6,16,576]{2,1,0:T(8,128)(2,1)} %collective-permute-done.2.refs_3_), channel_id=1, source_target_pairs={{0,32},{32,0},{1,33},{33,1},{2,34},{34,2},{3,35},{35,3},{4,36},{36... | collective-permute-start | bytes 331784 | tf_op jit(solution)/shard_map/ppermute | solution.py:33
  55.8 55.7 %all-to-all-start.1 = ((bf16[32,16,2048]{2,1,0:T(8,128)(2,1)}), bf16[32,16,2048]{2,1,0:T(8,128)(2,1)S(1)}, u32[]{:S(2)}, u32[]{:S(2)}) async-start(bf16[32,16,2048]{2,1,0:T(8,128)(2,1)} %broadcast_in_dim.28), calls=%async_computation.1 | async-start | bytes 4194304 | tf_op jit(solution)/shard_map/all_to_all | solution.py:318
  113.2 10.9 %all-to-all-start.2 = ((bf16[8,64,224]{2,1,0:T(8,128)(2,1)}), bf16[8,64,224]{2,1,0:T(8,128)(2,1)S(1)}, u32[]{:S(2)}, u32[]{:S(2)}) async-start(bf16[8,64,224]{2,1,0:T(8,128)(2,1)} %bitcast.6), calls=%async_computation.2 | async-start | bytes 524288 | tf_op jit(solution)/shard_map/all_to_all | solution.py:318
  125.1 20.2 %all-to-all-start.3 = ((bf16[32,24,224]{2,1,0:T(8,128)(2,1)}), bf16[32,24,224]{2,1,0:T(8,128)(2,1)S(1)}, u32[]{:S(2)}, u32[]{:S(2)}) async-start(bf16[32,24,224]{2,1,0:T(8,128)(2,1)} %get-tuple-element.18), calls=%async_computation.3 | async-start | bytes 786432 | tf_op jit(solution)/shard_map/all_to_all | solution.py:318
  145.6 9.5 %collective-permute-start.9 = (bf16[32,24,224]{2,1,0:T(8,128)(2,1)S(1)}, bf16[32,24,224]{2,1,0:T(8,128)(2,1)S(1)}, u32[]{:S(2)}, u32[]{:S(2)}) collective-permute-start(bf16[32,24,224]{2,1,0:T(8,128)(2,1)S(1)} %norm.1.refs_0_), channel_id=1, source_target_pairs={{0,192},{64,0},{128,64},{192,128},{1,193},{65,1},{129,65},{193,129... | collective-permute-start | bytes 1032200 | tf_op jit(solution)/shard_map/ppermute | solution.py:33
  146.8 9.6 %collective-permute-start.7 = (bf16[32,24,224]{2,1,0:T(8,128)(2,1)S(1)}, bf16[32,24,224]{2,1,0:T(8,128)(2,1)S(1)}, u32[]{:S(2)}, u32[]{:S(2)}) collective-permute-start(bf16[32,24,224]{2,1,0:T(8,128)(2,1)S(1)} %norm.1.refs_0_), channel_id=1, source_target_pairs={{0,64},{64,128},{128,192},{192,0},{1,65},{65,129},{129,193},{193,1... | collective-permute-start | bytes 1032200 | tf_op jit(solution)/shard_map/ppermute | solution.py:33
  147.7 15.7 %collective-permute-start.11 = (bf16[32,24,224]{2,1,0:T(8,128)(2,1)S(1)}, bf16[32,24,224]{2,1,0:T(8,128)(2,1)S(1)}, u32[]{:S(2)}, u32[]{:S(2)}) collective-permute-start(bf16[32,24,224]{2,1,0:T(8,128)(2,1)S(1)} %norm.1.refs_0_), channel_id=1, source_target_pairs={{0,32},{32,0},{1,33},{33,1},{2,34},{34,2},{3,35},{35,3},{4,36},{36... | collective-permute-start | bytes 1032200 | tf_op jit(solution)/shard_map/ppermute | solution.py:33
  155.1 5.7 %collective-permute-start.10 = (bf16[16,24,224]{2,1,0:T(8,128)(2,1)S(1)}, bf16[16,24,224]{2,1,0:T(8,128)(2,1)S(1)}, u32[]{:S(2)}, u32[]{:S(2)}) collective-permute-start(bf16[16,24,224]{2,1,0:T(8,128)(2,1)S(1)} %slice.48), channel_id=1, source_target_pairs={{0,192},{64,0},{128,64},{192,128},{1,193},{65,1},{129,65},{193,129... | collective-permute-start | bytes 516104 | tf_op jit(solution)/shard_map/ppermute | solution.py:33
  156.4 7.0 %collective-permute-start.8 = (bf16[16,24,224]{2,1,0:T(8,128)(2,1)S(1)}, bf16[16,24,224]{2,1,0:T(8,128)(2,1)S(1)}, u32[]{:S(2)}, u32[]{:S(2)}) collective-permute-start(bf16[16,24,224]{2,1,0:T(8,128)(2,1)S(1)} %slice.47), channel_id=1, source_target_pairs={{0,64},{64,128},{128,192},{192,0},{1,65},{65,129},{129,193},{193,1... | collective-permute-start | bytes 516104 | tf_op jit(solution)/shard_map/ppermute | solution.py:33
  157.4 6.0 %collective-permute-start.15 = (bf16[32,24,224]{2,1,0:T(8,128)(2,1)S(1)}, bf16[32,24,224]{2,1,0:T(8,128)(2,1)S(1)}, u32[]{:S(2)}, u32[]{:S(2)}) collective-permute-start(bf16[32,24,224]{2,1,0:T(8,128)(2,1)S(1)} %collective-permute-done.9.refs_4_), channel_id=1, source_target_pairs={{0,32},{32,0},{1,33},{33,1},{2,34},{34,2},{3,35},{35,3},{4,36},{36... | collective-permute-start | bytes 1032200 | tf_op jit(solution)/shard_map/ppermute | solution.py:33
  157.4 7.5 %collective-permute-start.12 = (bf16[32,24,224]{2,1,0:T(8,128)(2,1)S(1)}, bf16[32,24,224]{2,1,0:T(8,128)(2,1)S(1)}, u32[]{:S(2)}, u32[]{:S(2)}) collective-permute-start(bf16[32,24,224]{2,1,0:T(8,128)(2,1)S(1)} %collective-permute-done.7.refs_1_), channel_id=1, source_target_pairs={{0,32},{32,0},{1,33},{33,1},{2,34},{34,2},{3,35},{35,3},{4,36},{36... | collective-permute-start | bytes 1032200 | tf_op jit(solution)/shard_map/ppermute | solution.py:33
  160.9 2.5 %collective-permute-start.14 = (bf16[16,24,224]{2,1,0:T(8,128)(2,1)S(1)}, bf16[16,24,224]{2,1,0:T(8,128)(2,1)S(1)}, u32[]{:S(2)}, u32[]{:S(2)}) collective-permute-start(bf16[16,24,224]{2,1,0:T(8,128)(2,1)S(1)} %collective-permute-done.10.refs_3_), channel_id=1, source_target_pairs={{0,32},{32,0},{1,33},{33,1},{2,34},{34,2},{3,35},{35,3},{4,36},{36... | collective-permute-start | bytes 516104 | tf_op jit(solution)/shard_map/ppermute | solution.py:33
  171.7 2.9 %collective-permute-start.18 = (bf16[32,24,224]{2,1,0:T(8,128)(2,1)S(1)}, bf16[32,24,224]{2,1,0:T(8,128)(2,1)S(1)}, u32[]{:S(2)}, u32[]{:S(2)}) collective-permute-start(bf16[32,24,224]{2,1,0:T(8,128)(2,1)S(1)} %get-tuple-element.24), channel_id=1, source_target_pairs={{0,32},{32,0},{1,33},{33,1},{2,34},{34,2},{3,35},{35,3},{4,36},{36... | collective-permute-start | bytes 1032200 | tf_op jit(solution)/shard_map/ppermute | solution.py:33
  172.1 12.1 %collective-permute-start.16 = (bf16[32,24,224]{2,1,0:T(8,128)(2,1)S(1)}, bf16[32,24,224]{2,1,0:T(8,128)(2,1)S(1)}, u32[]{:S(2)}, u32[]{:S(2)}) collective-permute-start(bf16[32,24,224]{2,1,0:T(8,128)(2,1)S(1)} %get-tuple-element.20), channel_id=1, source_target_pairs={{0,32},{32,0},{1,33},{33,1},{2,34},{34,2},{3,35},{35,3},{4,36},{36... | collective-permute-start | bytes 1032200 | tf_op jit(solution)/shard_map/ppermute | solution.py:33
  172.2 4.6 %collective-permute-start.21 = (bf16[32,24,224]{2,1,0:T(8,128)(2,1)S(1)}, bf16[32,24,224]{2,1,0:T(8,128)(2,1)S(1)}, u32[]{:S(2)}, u32[]{:S(2)}) collective-permute-start(bf16[32,24,224]{2,1,0:T(8,128)(2,1)S(1)} %get-tuple-element.26), channel_id=1, source_target_pairs={{0,32},{32,0},{1,33},{33,1},{2,34},{34,2},{3,35},{35,3},{4,36},{36... | collective-permute-start | bytes 1032200 | tf_op jit(solution)/shard_map/ppermute | solution.py:33
  174.7 7.0 %collective-permute-start.19 = (bf16[16,24,224]{2,1,0:T(8,128)(2,1)S(1)}, bf16[16,24,224]{2,1,0:T(8,128)(2,1)S(1)}, u32[]{:S(2)}, u32[]{:S(2)}) collective-permute-start(bf16[16,24,224]{2,1,0:T(8,128)(2,1)S(1)} %get-tuple-element.31), channel_id=1, source_target_pairs={{0,192},{64,0},{128,64},{192,128},{1,193},{65,1},{129,65},{193,129... | collective-permute-start | bytes 516104 | tf_op jit(solution)/shard_map/ppermute | solution.py:33
  175.0 8.5 %collective-permute-start.22 = (bf16[16,24,224]{2,1,0:T(8,128)(2,1)S(1)}, bf16[16,24,224]{2,1,0:T(8,128)(2,1)S(1)}, u32[]{:S(2)}, u32[]{:S(2)}) collective-permute-start(bf16[16,24,224]{2,1,0:T(8,128)(2,1)S(1)} %get-tuple-element.32), channel_id=1, source_target_pairs={{0,64},{64,128},{128,192},{192,0},{1,65},{65,129},{129,193},{193,1... | collective-permute-start | bytes 516104 | tf_op jit(solution)/shard_map/ppermute | solution.py:33
  181.9 10.4 %collective-permute-start.20 = (bf16[32,24,224]{2,1,0:T(8,128)(2,1)S(1)}, bf16[32,24,224]{2,1,0:T(8,128)(2,1)S(1)}, u32[]{:S(2)}, u32[]{:S(2)}) collective-permute-start(bf16[32,24,224]{2,1,0:T(8,128)(2,1)S(1)} %pad_maximum_fusion), channel_id=1, source_target_pairs={{0,192},{64,0},{128,64},{192,128},{1,193},{65,1},{129,65},{193,129... | collective-permute-start | bytes 1032200 | tf_op jit(solution)/shard_map/ppermute | solution.py:33
  183.6 11.5 %collective-permute-start.23 = (bf16[32,24,224]{2,1,0:T(8,128)(2,1)S(1)}, bf16[32,24,224]{2,1,0:T(8,128)(2,1)S(1)}, u32[]{:S(2)}, u32[]{:S(2)}) collective-permute-start(bf16[32,24,224]{2,1,0:T(8,128)(2,1)S(1)} %pad_maximum_fusion.1), channel_id=1, source_target_pairs={{0,64},{64,128},{128,192},{192,0},{1,65},{65,129},{129,193},{193,1... | collective-permute-start | bytes 1032200 | tf_op jit(solution)/shard_map/ppermute | solution.py:33
  (14 other events, 236.4 us)
where the time goes:
time: 217 us; the launch traced here: 216 us
  waiting for transfers between devices  120 us (55%)
  starting transfers between devices  41.5 us (19%)
  blocking collectives  19.5 us (9%)
  Pallas kernels  18.2 us (8%)
  local copies, waits for them, and re-layouts  7.49 us (3%)
  matrix products  5.96 us (3%)
  other arithmetic  2.64 us (1%)
    all_to_all x4, waiting for transfers between devices, exchange(): return lax.all_to_all(x, axes, split_axis=0, concat_axis=0, tiled=True)  85.9 us
    ppermute x24, waiting for transfers between devices, shifted(): return lax.ppermute(x, axis, [(i, (i + step) % n) for i in range(n)])  34.4 us
    all_to_all x4, starting transfers between devices, exchange(): return lax.all_to_all(x, axes, split_axis=0, concat_axis=0, tiled=True)  26.4 us
    all_to_all x1, blocking collectives, exchange(): return lax.all_to_all(x, axes, split_axis=0, concat_axis=0, tiled=True)  19.5 us
    ppermute x24, starting transfers between devices, shifted(): return lax.ppermute(x, axis, [(i, (i + step) % n) for i in range(n)])  15.1 us
    pallas_call x1, Pallas kernels, run_experts(): pl.pallas_call(functools.partial(experts_kernel, layout), out_shape=tuple...  6.72 us
    pallas_call x1, Pallas kernels, new_attention(): pl.pallas_call(new_attention_kernel, out_shape=jax.ShapeDtypeStruct((rows...  5.66 us
  transfers between devices with their start and end apart: 28, of which 15 were waited for; matrix products, arithmetic and copies ran while one was open for 5% of the time, Pallas kernels for 0%

commit v1 on v0

--- a/solution.py
+++ b/solution.py
@@ -33,16 +33,18 @@
     return lax.ppermute(x, axis, [(i, (i + step) % n) for i in range(n)])
 
 
-def ring_gather(x, axis):
+def ring_gather(x, axis, dim):
     n = lax.axis_size(axis)
     far = n // 2
-    cut = x.shape[0] // 2
+    cut = x.shape[dim] // 2
     found = {0: x}
     right, left = x, x
     for step in range(1, far):
         right, left = shifted(right, axis, 1), shifted(left, axis, -1)
         found[step], found[n - step] = right, left
-    found[far] = (shifted(right[:cut], axis, 1), shifted(left[cut:], axis, -1))
+    low = lax.slice_in_dim(right, 0, cut, axis=dim)
+    high = lax.slice_in_dim(left, cut, x.shape[dim], axis=dim)
+    found[far] = (shifted(low, axis, 1), shifted(high, axis, -1))
     return [found[d] for d in range(n)]
 
 
@@ -172,6 +174,44 @@
     )(lens, at, queries, value_up, resident, *pieces)
 
 
+def stack_kernel(*refs):
+    rows = refs[0].shape[0]
+    for k, ref in enumerate(refs[:-1]):
+        refs[-1][k * rows : (k + 1) * rows, :] = ref[...]
+
+
+def stacked(pieces):
+    rows, width = pieces[0].shape
+    return pl.pallas_call(
+        stack_kernel,
+        out_shape=jax.ShapeDtypeStruct((rows * len(pieces), width), pieces[0].dtype),
+        in_specs=[whole()] * len(pieces),
+        out_specs=whole(),
+        compiler_params=params(),
+        name="stack",
+    )(*pieces)
+
+
+def project_kernel(makers, w_ref, *refs):
+    pieces, out_ref = refs[:-1], refs[-1]
+    rows = out_ref.shape[1]
+    attention = jnp.concatenate([piece[...] for piece in pieces], axis=0)
+    mixed = lax.dot_general(attention, w_ref[...], (((1,), (1,)), ((), ())), preferred_element_type=F32).astype(BF)
+    for k in range(out_ref.shape[0]):
+        out_ref[makers[k]] = mixed[k * rows : (k + 1) * rows]
+
+
+def project(makers, w_output_t, pieces, rows):
+    return pl.pallas_call(
+        project_kernel,
+        out_shape=jax.ShapeDtypeStruct((makers.shape[0], rows, w_output_t.shape[0]), BF),
+        in_specs=[whole(pltpu.SMEM)] + [whole()] * (1 + len(pieces)),
+        out_specs=whole(),
+        compiler_params=params(),
+        name="project",
+    )(makers, w_output_t, *pieces)
+
+
 def plan_kernel(rows_dev, ids_ref, gates_ref, sel_ref, mix_ref):
     rows, choose = ids_ref.shape
     slots_all = sel_ref.shape[1]
@@ -244,17 +284,21 @@
 
 
 def norm_kernel(x_ref, gain_ref, out_ref):
-    x = x_ref[...].astype(F32)
-    width = x.shape[0] * x.shape[2]
-    squares = jnp.sum(jnp.sum(x * x, axis=0), axis=1, keepdims=True)
-    inverse = lax.rsqrt(squares / width + 1e-06)
-    out_ref[...] = (x * inverse[None] * gain_ref[...].astype(F32)).astype(BF)
+    count = x_ref.shape[0]
+    squares = 0.0
+    for j in range(count):
+        x = x_ref[j].astype(F32)
+        squares = squares + x * x
+    mean = jnp.sum(squares, axis=1, keepdims=True) / out_ref.shape[1]
+    inverse = lax.rsqrt(mean + 1e-06)
+    x = jnp.concatenate([x_ref[j].astype(F32) for j in range(count)], axis=1)
+    out_ref[...] = (x * inverse * gain_ref[...].astype(F32)).astype(BF)
 
 
 def normed_rows(x, gain):
     return pl.pallas_call(
         norm_kernel,
-        out_shape=jax.ShapeDtypeStruct(x.shape, BF),
+        out_shape=jax.ShapeDtypeStruct((x.shape[1], x.shape[0] * x.shape[2]), BF),
         in_specs=[whole()] * 2,
         out_specs=whole(),
         compiler_params=params(),
@@ -265,36 +309,48 @@
 def experts_kernel(layout, *refs):
     count = sum(layout)
     x_refs, (gate_ref, up_ref, down_ref), outs = refs[:count], refs[count : count + 3], refs[count + 3 :]
-    columns, slots = x_refs[0].shape[0], x_refs[0].shape[1]
-    width = x_refs[0].shape[2]
-    gate = up = None
-    for j in range(columns):
-        pieces, at = [], 0
-        for parts in layout:
-            split = columns // parts
-            pieces.append(x_refs[at + j // split][j % split].astype(F32))
-            at += parts
-        x = jnp.concatenate(pieces, axis=0).astype(BF)
-        g = jnp.dot(x, gate_ref[j], preferred_element_type=F32)
-        u = jnp.dot(x, up_ref[j], preferred_element_type=F32)
-        gate, up = (g, u) if gate is None else (gate + g, up + u)
+    slots = x_refs[0].shape[0]
+    blocks, at = [], 0
+    for parts in layout:
+        blocks.append(jnp.concatenate([x_refs[at + p][...] for p in range(parts)], axis=1))
+        at += parts
+    x = jnp.concatenate(blocks, axis=0)
+    gate = jnp.dot(x, gate_ref[...], preferred_element_type=F32)
+    up = jnp.dot(x, up_ref[...], preferred_element_type=F32)
     act = (gate * jax.nn.sigmoid(gate) * up).astype(BF)
-    for j in range(columns):
-        y = jnp.dot(act, down_ref[:, j * width : (j + 1) * width], preferred_element_type=F32)
-        for k, out in enumerate(outs):
-            out[j] = y[k * slots : (k + 1) * slots].astype(out.dtype)
-
-
-def run_experts(layout, pieces, w_gate, w_up, w_down, types):
-    shape = pieces[0].shape
+    y = jnp.dot(act, down_ref[...], preferred_element_type=F32)
+    for k, out in enumerate(outs):
+        out[...] = y[k * slots : (k + 1) * slots].astype(BF)
+
+
+def run_experts(layout, pieces, w_gate, w_up, w_down):
+    out = jax.ShapeDtypeStruct(pieces[0].shape, BF)
     return pl.pallas_call(
         functools.partial(experts_kernel, layout),
-        out_shape=tuple(jax.ShapeDtypeStruct(shape, kind) for kind in types),
+        out_shape=(out,) * len(layout),
         in_specs=[whole()] * (len(pieces) + 3),
-        out_specs=tuple(whole() for _ in types),
+        out_specs=(whole(),) * len(layout),
         compiler_params=params(),
         name="experts",
     )(*pieces, w_gate, w_up, w_down)
+
+
+def total_kernel(kept_ref, after_ref, before_ref, out_ref):
+    width = out_ref.shape[2]
+    total = kept_ref[...] + after_ref[...].astype(F32) + before_ref[...].astype(F32)
+    for j in range(out_ref.shape[0]):
+        out_ref[j] = total[:, j * width : (j + 1) * width].astype(BF)
+
+
+def total_by_columns(kept, after, before, parts):
+    return pl.pallas_call(
+        total_kernel,
+        out_shape=jax.ShapeDtypeStruct((parts, kept.shape[0], kept.shape[1] // parts), BF),
+        in_specs=[whole()] * 3,
+        out_specs=whole(),
+        compiler_params=params(),
+        name="total",
+    )(kept, after, before)
 
 
 def combine_kernel(back_ref, mix_ref, hidden_ref, out_ref):
@@ -319,26 +375,23 @@
 
 
 def gather_over_head(x):
-    near = ring_gather(x, HEAD[0])
+    near = ring_gather(x, HEAD[0], 1)
     layout = [len(p) if isinstance(p, tuple) else 1 for p in near]
     near = flat(near)
     far = [shifted(p, HEAD[1], 1) for p in near]
-    return layout * 2, near + far
-
-
-def sum_over_head(kept, sent):
-    other = [shifted(s, HEAD[1], 1) for s in (sent[2], sent[1], sent[3], sent[0])]
-    other = [other[3], other[1], other[0], other[2]]
-    pair = [k + o.astype(F32) for k, o in zip(kept, other)]
-    cut = pair[2].shape[0] // 2
+    return tuple(layout * 2), near + far
+
+
+def sum_over_head(kept, sent, parts):
+    other = {d: shifted(sent[d], HEAD[1], 1) for d in (2, 1, 3, 0)}
+    pair = [kept[d].astype(F32) + other[d].astype(F32) for d in range(4)]
+    cut = pair[2].shape[1] // 2
     far = pair[2].astype(BF)
-    low = shifted(far[:cut], HEAD[0], -1).astype(F32)
-    high = shifted(far[cut:], HEAD[0], 1).astype(F32)
-    before = jnp.concatenate([pair[1][:cut] + low, pair[1][cut:]], axis=0).astype(BF)
-    after = jnp.concatenate([pair[3][:cut], pair[3][cut:] + high], axis=0).astype(BF)
-    from_after = shifted(before, HEAD[0], -1).astype(F32)
-    from_before = shifted(after, HEAD[0], 1).astype(F32)
-    return (pair[0] + from_after + from_before).astype(BF)
+    low = shifted(far[:, :cut], HEAD[0], -1).astype(F32)
+    high = shifted(far[:, cut:], HEAD[0], 1).astype(F32)
+    before = jnp.concatenate([pair[1][:, :cut] + low, pair[1][:, cut:]], axis=1).astype(BF)
+    after = jnp.concatenate([pair[3][:, :cut], pair[3][:, cut:] + high], axis=1).astype(BF)
+    return total_by_columns(pair[0], shifted(before, HEAD[0], -1), shifted(after, HEAD[0], 1), parts)
 
 
 def per_device(
@@ -360,6 +413,8 @@
 ):
     n_expert = lax.axis_size(EXPERT)
     n_head = lax.axis_size(HEAD)
+    n_z, n_y = lax.axis_size(EXPERT[0]), lax.axis_size(EXPERT[1])
+    z, y = lax.axis_index(EXPERT[0]), lax.axis_index(EXPERT[1])
     me = lax.axis_index(EXPERT)
     head = lax.axis_index(HEAD)
     req_count = resident_cache.shape[0]
@@ -390,26 +445,21 @@
     resident = attend(queries[:req_count], jnp.swapaxes(resident_cache, 1, 2), resident_len, value_up)
     attention = new_attention(lens, at, queries, value_up, resident, pieces)
 
-    everywhere = exchange(jnp.broadcast_to(attention[None], (n_expert,) + attention.shape), EXPERT)
-    mixed = jnp.dot(everywhere.reshape(rows_all, -1), w_output, preferred_element_type=F32).astype(BF)
+    along_y = [attention] + [shifted(attention, EXPERT[1], d) for d in range(1, n_y)]
+    rows_here = flat(ring_gather(stacked(along_y), EXPERT[0], 0))
+    away = jnp.arange(n_expert, dtype=I32)
+    makers = ((z + n_z - (away // n_y)) % n_z) * n_y + (y + n_y - away % n_y) % n_y
+    mixed = project(makers, w_output.T, rows_here, rows_dev)
     parts = exchange(mixed.reshape(n_head, block_rows, columns), HEAD)
 
     block = lambda a: lax.dynamic_slice_in_dim(a, head * block_rows, block_rows)
     sel, mix = plan(block(expert_ids), block(expert_gates), rows_dev, n_expert)
     hidden, outgoing = dispatch(parts, block(residual), sel, n_expert)
     received = exchange(outgoing, EXPERT)
-    normed = normed_rows(received, norm_gain.reshape(n_expert, 1, columns))
+    normed = normed_rows(received, norm_gain.reshape(1, -1))
     layout, pieces = gather_over_head(normed)
-    x_count = lax.axis_size(HEAD[0])
-    made = run_experts(
-        tuple(layout),
-        pieces,
-        w_gate.reshape(n_expert, columns, -1),
-        w_up.reshape(n_expert, columns, -1),
-        w_down.reshape(w_down.shape[1:]),
-        [F32] * x_count + [BF] * x_count,
-    )
-    summed = sum_over_head(made[:x_count], made[x_count:])
+    made = run_experts(layout, pieces, *(w.reshape(w.shape[1:]) for w in (w_gate, w_up, w_down)))
+    summed = sum_over_head(made[:ring], made[ring:], n_expert)
     back = exchange(summed, EXPERT)
     return combine(back, mix, hidden)
 

time: 217 us -> 196 us (0.903)
  waiting for transfers between devices: 120 us -> 95.7 us
  starting transfers between devices: 41.5 us -> 53 us
  matrix products: 5.96 us -> 3.69 us
  local copies, waits for them, and re-layouts: 7.49 us -> 5.31 us
    all_to_all x4 -> x3, waiting for transfers between devices: 85.9 us -> 37.5 us  [exchange(): return lax.all_to_all(x, axes, split_axis=0, concat_axis=0, tiled=True)]
    ppermute x24 -> x35, waiting for transfers between devices: 34.4 us -> 58.1 us  [shifted(): return lax.ppermute(x, axis, [(i, (i + step) % n) for i in range(n)])]
    ppermute x24 -> x35, starting transfers between devices: 15.1 us -> 29.5 us  [shifted(): return lax.ppermute(x, axis, [(i, (i + step) % n) for i in range(n)])]
    all_to_all x4 -> x3, starting transfers between devices: 26.4 us -> 23.5 us  [exchange(): return lax.all_to_all(x, axes, split_axis=0, concat_axis=0, tiled=True)]
    pallas_call x2 -> x5, Pallas kernels: 7 us -> 7.39 us  [the longest x1 5 us: run_experts(): pl.pallas_call(functools.partial(experts_kernel, layout), out_shape=(out,...]
  transfers between devices with their start and end apart: 28 -> 38, of which waited for: 15 -> 25; matrix products, arithmetic and copies ran while one was open for 5% -> 3% of each run, Pallas kernels for 0% -> 0%
where the time goes in v1:
time: 196 us; the launch traced here: 195 us
  waiting for transfers between devices  95.7 us (49%)
  starting transfers between devices  53 us (27%)
  blocking collectives  18.6 us (9%)
  Pallas kernels  17.5 us (9%)
  local copies, waits for them, and re-layouts  5.31 us (3%)
  matrix products  3.69 us (2%)
    ppermute x35, waiting for transfers between devices, shifted(): return lax.ppermute(x, axis, [(i, (i + step) % n) for i in range(n)])  58.1 us
    all_to_all x3, waiting for transfers between devices, exchange(): return lax.all_to_all(x, axes, split_axis=0, concat_axis=0, tiled=True)  37.5 us
    ppermute x35, starting transfers between devices, shifted(): return lax.ppermute(x, axis, [(i, (i + step) % n) for i in range(n)])  29.5 us
    all_to_all x3, starting transfers between devices, exchange(): return lax.all_to_all(x, axes, split_axis=0, concat_axis=0, tiled=True)  23.5 us
    all_to_all x1, blocking collectives, exchange(): return lax.all_to_all(x, axes, split_axis=0, concat_axis=0, tiled=True)  18.6 us
    pallas_call x1, Pallas kernels, new_attention(): pl.pallas_call(new_attention_kernel, out_shape=jax.ShapeDtypeStruct((rows...  5.18 us
    pallas_call x1, Pallas kernels, run_experts(): pl.pallas_call(functools.partial(experts_kernel, layout), out_shape=(out,...  5 us
  transfers between devices with their start and end apart: 38, of which 25 were waited for; matrix products, arithmetic and copies ran while one was open for 3% of the time, Pallas kernels for 0%

profile of v1, /device:TPU:32, one launch (start us, length us, event | category | flops | bytes accessed | tf_op | source)
XLA Modules:
  0.0 195.3 jit_solution(15331215039900071139)
XLA Ops:
  3.6 11.4 %all-to-all-start = ((bf16[32,16,576]{2,1,0:T(8,128)(2,1)}), bf16[32,16,576]{2,1,0:T(8,128)(2,1)S(1)}, u32[]{:S(2)}, u32[]{:S(2)}) async-start(bf16[32,16,576]{2,1,0:T(8,128)(2,1)} %pack_cache.1), calls=%async_computation | async-start | bytes 1310720 | tf_op jit(solution)/shard_map/all_to_all | solution.py:374
  17.4 17.4 %all-to-all-done.arrived_ref = bf16[32,16,576]{2,1,0:T(8,128)(2,1)S(1)} async-done(((bf16[32,16,576]{2,1,0:T(8,128)(2,1)}), bf16[32,16,576]{2,1,0:T(8,128)(2,1)S(1)}, u32[]{:S(2)}, u32[]{:S(2)}) %all-to-all-start) | async-done | bytes 589856 | tf_op jit(solution)/shard_map/all_to_all | solution.py:374
  35.6 2.8 %collective-permute-start.2 = (bf16[6,16,576]{2,1,0:T(8,128)(2,1)S(1)}, bf16[6,16,576]{2,1,0:T(8,128)(2,1)S(1)}, u32[]{:S(2)}, u32[]{:S(2)}) collective-permute-start(bf16[6,16,576]{2,1,0:T(8,128)(2,1)S(1)} %select_arrived.1.refs_0_), channel_id=1, source_target_pairs={{0,192},{64,0},{128,64},{192,128},{1,193},{65,1},{129,65},{193,129... | collective-permute-start | bytes 331784 | tf_op jit(solution)/shard_map/ppermute | solution.py:33
  42.2 2.6 %collective-permute-done.1.refs_2_ = bf16[6,16,576]{2,1,0:T(8,128)(2,1)S(1)} collective-permute-done((bf16[6,16,576]{2,1,0:T(8,128)(2,1)S(1)}, bf16[6,16,576]{2,1,0:T(8,128)(2,1)S(1)}, u32[]{:S(2)}, u32[]{:S(2)}) %collective-permute-start.1) | collective-permute-done | bytes 110624 | tf_op jit(solution)/shard_map/ppermute | solution.py:33
  47.4 5.2 %new_attention.1.refs_0_ = bf16[16,2048]{1,0:T(8,128)(2,1)S(1)} custom-call(s32[12]{0:T(128)S(1)} %get-tuple-element.30.lens, s32[2]{0:T(128)S(1)} %pad_add_fusion.at, bf16[16,16,576]{2,1,0:T(8,128)(2,1)S(1)} %copy-done.3, bf16[16,512,128]{2,1,0:T(8,128)(2,1)S(1)} %copy-done.1, bf16[4,2048]{1,0:T(4,128)(2,1)S(1)} %fusion.4.res_ref, ...), custom_call_target="tpu_custom_call" | custom-call | tf_op jit(solution)/shard_map/new_attention/pallas_call | solution.py:166
  52.6 2.0 %collective-permute-start.9 = (bf16[16,2048]{1,0:T(8,128)(2,1)S(1)}, bf16[16,2048]{1,0:T(8,128)(2,1)S(1)}, u32[]{:S(2)}, u32[]{:S(2)}) collective-permute-start(bf16[16,2048]{1,0:T(8,128)(2,1)S(1)} %new_attention.1.refs_0_), channel_id=1, source_target_pairs={{0,3},{1,0},{2,1},{3,2},{4,7},{5,4},{6,5},{7,6},{8,11},{9,8},{10,9... | collective-permute-start | bytes 196616 | tf_op jit(solution)/shard_map/ppermute | solution.py:33
  57.7 3.0 %collective-permute-done.8.refs_2_ = bf16[16,2048]{1,0:T(8,128)(2,1)S(1)} collective-permute-done((bf16[16,2048]{1,0:T(8,128)(2,1)S(1)}, bf16[16,2048]{1,0:T(8,128)(2,1)S(1)}, u32[]{:S(2)}, u32[]{:S(2)}) %collective-permute-start.8) | collective-permute-done | bytes 65568 | tf_op jit(solution)/shard_map/ppermute | solution.py:33
  63.5 5.7 %collective-permute-done.14.refs_8_ = bf16[64,2048]{1,0:T(8,128)(2,1)S(1)} collective-permute-done((bf16[64,2048]{1,0:T(8,128)(2,1)S(1)}, bf16[64,2048]{1,0:T(8,128)(2,1)S(1)}, u32[]{:S(2)}, u32[]{:S(2)}) %collective-permute-start.14) | collective-permute-done | bytes 262176 | tf_op jit(solution)/shard_map/ppermute | solution.py:33
  71.3 4.8 %collective-permute-done.15.refs_7_ = bf16[64,2048]{1,0:T(8,128)(2,1)S(1)} collective-permute-done((bf16[64,2048]{1,0:T(8,128)(2,1)S(1)}, bf16[64,2048]{1,0:T(8,128)(2,1)S(1)}, u32[]{:S(2)}, u32[]{:S(2)}) %collective-permute-start.15) | collective-permute-done | bytes 262176 | tf_op jit(solution)/shard_map/ppermute | solution.py:33
  78.1 5.1 %collective-permute-done.16.refs_6_ = bf16[64,2048]{1,0:T(8,128)(2,1)S(1)} collective-permute-done((bf16[64,2048]{1,0:T(8,128)(2,1)S(1)}, bf16[64,2048]{1,0:T(8,128)(2,1)S(1)}, u32[]{:S(2)}, u32[]{:S(2)}) %collective-permute-start.16) | collective-permute-done | bytes 262176 | tf_op jit(solution)/shard_map/ppermute | solution.py:33
  93.0 3.4 %all-to-all-start.1 = ((bf16[8,64,224]{2,1,0:T(8,128)(2,1)}), bf16[8,64,224]{2,1,0:T(8,128)(2,1)S(1)}, u32[]{:S(2)}, u32[]{:S(2)}) async-start(bf16[8,64,224]{2,1,0:T(8,128)(2,1)} %bitcast.6), calls=%async_computation.1 | async-start | bytes 524288 | tf_op jit(solution)/shard_map/all_to_all | solution.py:374
  98.1 5.8 %all-to-all-done.1.parts_ref = bf16[8,64,224]{2,1,0:T(8,128)(2,1)S(1)} async-done(((bf16[8,64,224]{2,1,0:T(8,128)(2,1)}), bf16[8,64,224]{2,1,0:T(8,128)(2,1)S(1)}, u32[]{:S(2)}, u32[]{:S(2)}) %all-to-all-start.1) | async-done | bytes 229408 | tf_op jit(solution)/shard_map/all_to_all | solution.py:374
  104.9 8.7 %all-to-all-start.2 = ((bf16[32,24,224]{2,1,0:T(8,128)(2,1)}), bf16[32,24,224]{2,1,0:T(8,128)(2,1)S(1)}, u32[]{:S(2)}, u32[]{:S(2)}) async-start(bf16[32,24,224]{2,1,0:T(8,128)(2,1)} %get-tuple-element.18), calls=%async_computation.2 | async-start | bytes 786432 | tf_op jit(solution)/shard_map/all_to_all | solution.py:374
  113.7 14.3 %all-to-all-done.2.x_ref = bf16[32,24,224]{2,1,0:T(8,128)(2,1)S(1)} async-done(((bf16[32,24,224]{2,1,0:T(8,128)(2,1)}), bf16[32,24,224]{2,1,0:T(8,128)(2,1)S(1)}, u32[]{:S(2)}, u32[]{:S(2)}) %all-to-all-start.2) | async-done | bytes 344096 | tf_op jit(solution)/shard_map/all_to_all | solution.py:374
  130.3 6.8 %collective-permute-done.20.refs_4_ = bf16[24,7168]{1,0:T(8,128)(2,1)S(1)} collective-permute-done((bf16[24,7168]{1,0:T(8,128)(2,1)S(1)}, bf16[24,7168]{1,0:T(8,128)(2,1)S(1)}, u32[]{:S(2)}, u32[]{:S(2)}) %collective-permute-start.20) | collective-permute-done | bytes 344096 | tf_op jit(solution)/shard_map/ppermute | solution.py:33
  139.8 2.8 %collective-permute-done.21.refs_3_ = bf16[24,3584]{1,0:T(8,128)(2,1)S(1)} collective-permute-done((bf16[24,3584]{1,0:T(8,128)(2,1)S(1)}, bf16[24,3584]{1,0:T(8,128)(2,1)S(1)}, u32[]{:S(2)}, u32[]{:S(2)}) %collective-permute-start.21) | collective-permute-done | bytes 172064 | tf_op jit(solution)/shard_map/ppermute | solution.py:33
  142.6 2.5 %collective-permute-done.19.refs_2_ = bf16[24,3584]{1,0:T(8,128)(2,1)S(1)} collective-permute-done((bf16[24,3584]{1,0:T(8,128)(2,1)S(1)}, bf16[24,3584]{1,0:T(8,128)(2,1)S(1)}, u32[]{:S(2)}, u32[]{:S(2)}) %collective-permute-start.19) | collective-permute-done | bytes 172064 | tf_op jit(solution)/shard_map/ppermute | solution.py:33
  146.6 5.0 %experts.1 = (bf16[24,7168]{1,0:T(8,128)(2,1)S(1)}, bf16[24,7168]{1,0:T(8,128)(2,1)S(1)}, bf16[24,7168]{1,0:T(8,128)(2,1)S(1)}, bf16[24,7168]{1,0:T(8,128)(2,1)S...) custom-call(bf16[24,7168]{1,0:T(8,128)(2,1)S(1)} %norm.1.refs_0_, ...), custom_call_target="tpu_custom_call" | custom-call | tf_op jit(solution)/shard_map/experts/pallas_call | solution.py:328
  154.5 3.2 %collective-permute-start.30 = (bf16[24,3584]{1,0:T(8,128)(2,1)S(1)}, bf16[24,3584]{1,0:T(8,128)(2,1)S(1)}, u32[]{:S(2)}, u32[]{:S(2)}) collective-permute-start(bf16[24,3584]{1,0:T(8,128)(2,1)S(1)} %get-tuple-element.32), channel_id=1, source_target_pairs={{0,192},{64,0},{128,64},{192,128},{1,193},{65,1},{129,65},{193,129... | collective-permute-start | bytes 516104 | tf_op jit(solution)/shard_map/ppermute | solution.py:33
  157.9 3.6 %collective-permute-done.30 = bf16[24,3584]{1,0:T(8,128)(2,1)S(1)} collective-permute-done((bf16[24,3584]{1,0:T(8,128)(2,1)S(1)}, bf16[24,3584]{1,0:T(8,128)(2,1)S(1)}, u32[]{:S(2)}, u32[]{:S(2)}) %collective-permute-start.30) | collective-permute-done | bytes 172064 | tf_op jit(solution)/shard_map/ppermute | solution.py:33
  161.5 3.8 %collective-permute-start.31 = (bf16[24,7168]{1,0:T(8,128)(2,1)S(1)}, bf16[24,7168]{1,0:T(8,128)(2,1)S(1)}, u32[]{:S(2)}, u32[]{:S(2)}) collective-permute-start(bf16[24,7168]{1,0:T(8,128)(2,1)S(1)} %pad_maximum_fusion), channel_id=1, source_target_pairs={{0,192},{64,0},{128,64},{192,128},{1,193},{65,1},{129,65},{193,129... | collective-permute-start | bytes 1032200 | tf_op jit(solution)/shard_map/ppermute | solution.py:33
  165.5 6.2 %collective-permute-done.31.after_ref = bf16[24,7168]{1,0:T(8,128)(2,1)S(1)} collective-permute-done((bf16[24,7168]{1,0:T(8,128)(2,1)S(1)}, bf16[24,7168]{1,0:T(8,128)(2,1)S(1)}, u32[]{:S(2)}, u32[]{:S(2)}) %collective-permute-start.31) | collective-permute-done | bytes 344096 | tf_op jit(solution)/shard_map/ppermute | solution.py:33
  171.7 3.6 %collective-permute-done.34.before_ref = bf16[24,7168]{1,0:T(8,128)(2,1)S(1)} collective-permute-done((bf16[24,7168]{1,0:T(8,128)(2,1)S(1)}, bf16[24,7168]{1,0:T(8,128)(2,1)S(1)}, u32[]{:S(2)}, u32[]{:S(2)}) %collective-permute-start.34) | collective-permute-done | bytes 344096 | tf_op jit(solution)/shard_map/ppermute | solution.py:33
  175.5 18.6 %all_to_all.20.back_ref = bf16[32,24,224]{2,1,0:T(8,128)(2,1)S(1)} all-to-all(bf16[32,24,224]{2,1,0:T(8,128)(2,1)S(1)} %total.1), channel_id=1, replica_groups=mesh['head_0'=4,'head_1'=2,'expert_0'=8,'expert_1'=4] {'expert_0','exper..., dimensions={0} | all-to-all | bytes 688128 | tf_op jit(solution)/shard_map/all_to_all | solution.py:374
  (117 shorter events, 46.7 us)
Async XLA Ops:
  3.6 31.2 %all-to-all-start = ((bf16[32,16,576]{2,1,0:T(8,128)(2,1)}), bf16[32,16,576]{2,1,0:T(8,128)(2,1)S(1)}, u32[]{:S(2)}, u32[]{:S(2)}) async-start(bf16[32,16,576]{2,1,0:T(8,128)(2,1)} %pack_cache.1), calls=%async_computation | async-start | bytes 1310720 | tf_op jit(solution)/shard_map/all_to_all | solution.py:374
  35.6 6.2 %collective-permute-start.2 = (bf16[6,16,576]{2,1,0:T(8,128)(2,1)S(1)}, bf16[6,16,576]{2,1,0:T(8,128)(2,1)S(1)}, u32[]{:S(2)}, u32[]{:S(2)}) collective-permute-start(bf16[6,16,576]{2,1,0:T(8,128)(2,1)S(1)} %select_arrived.1.refs_0_), channel_id=1, source_target_pairs={{0,192},{64,0},{128,64},{192,128},{1,193},{65,1},{129,65},{193,129... | collective-permute-start | bytes 331784 | tf_op jit(solution)/shard_map/ppermute | solution.py:33
  38.4 6.5 %collective-permute-start.1 = (bf16[6,16,576]{2,1,0:T(8,128)(2,1)S(1)}, bf16[6,16,576]{2,1,0:T(8,128)(2,1)S(1)}, u32[]{:S(2)}, u32[]{:S(2)}) collective-permute-start(bf16[6,16,576]{2,1,0:T(8,128)(2,1)S(1)} %select_arrived.1.refs_0_), channel_id=1, source_target_pairs={{0,128},{64,192},{128,0},{192,64},{1,129},{65,193},{129,1},{193,65... | collective-permute-start | bytes 331784 | tf_op jit(solution)/shard_map/ppermute | solution.py:33
  39.2 6.9 %collective-permute-start = (bf16[6,16,576]{2,1,0:T(8,128)(2,1)S(1)}, bf16[6,16,576]{2,1,0:T(8,128)(2,1)S(1)}, u32[]{:S(2)}, u32[]{:S(2)}) collective-permute-start(bf16[6,16,576]{2,1,0:T(8,128)(2,1)S(1)} %select_arrived.1.refs_0_), channel_id=1, source_target_pairs={{0,64},{64,128},{128,192},{192,0},{1,65},{65,129},{129,193},{193,1... | collective-permute-start | bytes 331784 | tf_op jit(solution)/shard_map/ppermute | solution.py:33
  55.2 6.2 %collective-permute-start.7 = (bf16[16,2048]{1,0:T(8,128)(2,1)S(1)}, bf16[16,2048]{1,0:T(8,128)(2,1)S(1)}, u32[]{:S(2)}, u32[]{:S(2)}) collective-permute-start(bf16[16,2048]{1,0:T(8,128)(2,1)S(1)} %new_attention.1.refs_0_), channel_id=1, source_target_pairs={{0,1},{1,2},{2,3},{3,0},{4,5},{5,6},{6,7},{7,4},{8,9},{9,10},{10,1... | collective-permute-start | bytes 196616 | tf_op jit(solution)/shard_map/ppermute | solution.py:33
  61.4 7.8 %collective-permute-start.14 = (bf16[64,2048]{1,0:T(8,128)(2,1)S(1)}, bf16[64,2048]{1,0:T(8,128)(2,1)S(1)}, u32[]{:S(2)}, u32[]{:S(2)}) collective-permute-start(bf16[64,2048]{1,0:T(8,128)(2,1)S(1)} %stack.13.refs_0_), channel_id=1, source_target_pairs={{0,28},{4,0},{8,4},{12,8},{16,12},{20,16},{24,20},{28,24},{1,29},{... | collective-permute-start | bytes 786440 | tf_op jit(solution)/shard_map/ppermute | solution.py:33
  62.7 7.2 %collective-permute-start.10 = (bf16[64,2048]{1,0:T(8,128)(2,1)S(1)}, bf16[64,2048]{1,0:T(8,128)(2,1)S(1)}, u32[]{:S(2)}, u32[]{:S(2)}) collective-permute-start(bf16[64,2048]{1,0:T(8,128)(2,1)S(1)} %stack.13.refs_0_), channel_id=1, source_target_pairs={{0,4},{4,8},{8,12},{12,16},{16,20},{20,24},{24,28},{28,0},{1,5},{5... | collective-permute-start | bytes 786440 | tf_op jit(solution)/shard_map/ppermute | solution.py:33
  69.2 6.8 %collective-permute-start.15 = (bf16[64,2048]{1,0:T(8,128)(2,1)S(1)}, bf16[64,2048]{1,0:T(8,128)(2,1)S(1)}, u32[]{:S(2)}, u32[]{:S(2)}) collective-permute-start(bf16[64,2048]{1,0:T(8,128)(2,1)S(1)} %collective-permute-done.14.refs_8_), channel_id=1, source_target_pairs={{0,28},{4,0},{8,4},{12,8},{16,12},{20,16},{24,20},{28,24},{1,29},{... | collective-permute-start | bytes 786440 | tf_op jit(solution)/shard_map/ppermute | solution.py:33
  69.9 6.4 %collective-permute-start.11 = (bf16[64,2048]{1,0:T(8,128)(2,1)S(1)}, bf16[64,2048]{1,0:T(8,128)(2,1)S(1)}, u32[]{:S(2)}, u32[]{:S(2)}) collective-permute-start(bf16[64,2048]{1,0:T(8,128)(2,1)S(1)} %collective-permute-done.10.refs_1_), channel_id=1, source_target_pairs={{0,4},{4,8},{8,12},{12,16},{16,20},{20,24},{24,28},{28,0},{1,5},{5... | collective-permute-start | bytes 786440 | tf_op jit(solution)/shard_map/ppermute | solution.py:33
  76.0 7.1 %collective-permute-start.16 = (bf16[64,2048]{1,0:T(8,128)(2,1)S(1)}, bf16[64,2048]{1,0:T(8,128)(2,1)S(1)}, u32[]{:S(2)}, u32[]{:S(2)}) collective-permute-start(bf16[64,2048]{1,0:T(8,128)(2,1)S(1)} %collective-permute-done.15.refs_7_), channel_id=1, source_target_pairs={{0,28},{4,0},{8,4},{12,8},{16,12},{20,16},{24,20},{28,24},{1,29},{... | collective-permute-start | bytes 786440 | tf_op jit(solution)/shard_map/ppermute | solution.py:33
  76.3 7.2 %collective-permute-start.12 = (bf16[64,2048]{1,0:T(8,128)(2,1)S(1)}, bf16[64,2048]{1,0:T(8,128)(2,1)S(1)}, u32[]{:S(2)}, u32[]{:S(2)}) collective-permute-start(bf16[64,2048]{1,0:T(8,128)(2,1)S(1)} %collective-permute-done.11.refs_2_), channel_id=1, source_target_pairs={{0,4},{4,8},{8,12},{12,16},{16,20},{20,24},{24,28},{28,0},{1,5},{5... | collective-permute-start | bytes 786440 | tf_op jit(solution)/shard_map/ppermute | solution.py:33
  83.5 6.3 %collective-permute-start.13 = (bf16[32,2048]{1,0:T(8,128)(2,1)S(1)}, bf16[32,2048]{1,0:T(8,128)(2,1)S(1)}, u32[]{:S(2)}, u32[]{:S(2)}) collective-permute-start(bf16[32,2048]{1,0:T(8,128)(2,1)S(1)} %slice.55), channel_id=1, source_target_pairs={{0,4},{4,8},{8,12},{12,16},{16,20},{20,24},{24,28},{28,0},{1,5},{5... | collective-permute-start | bytes 393224 | tf_op jit(solution)/shard_map/ppermute | solution.py:33
  93.0 10.9 %all-to-all-start.1 = ((bf16[8,64,224]{2,1,0:T(8,128)(2,1)}), bf16[8,64,224]{2,1,0:T(8,128)(2,1)S(1)}, u32[]{:S(2)}, u32[]{:S(2)}) async-start(bf16[8,64,224]{2,1,0:T(8,128)(2,1)} %bitcast.6), calls=%async_computation.1 | async-start | bytes 524288 | tf_op jit(solution)/shard_map/all_to_all | solution.py:374
  104.9 23.0 %all-to-all-start.2 = ((bf16[32,24,224]{2,1,0:T(8,128)(2,1)}), bf16[32,24,224]{2,1,0:T(8,128)(2,1)S(1)}, u32[]{:S(2)}, u32[]{:S(2)}) async-start(bf16[32,24,224]{2,1,0:T(8,128)(2,1)} %get-tuple-element.18), calls=%async_computation.2 | async-start | bytes 786432 | tf_op jit(solution)/shard_map/all_to_all | solution.py:374
  128.2 8.9 %collective-permute-start.20 = (bf16[24,7168]{1,0:T(8,128)(2,1)S(1)}, bf16[24,7168]{1,0:T(8,128)(2,1)S(1)}, u32[]{:S(2)}, u32[]{:S(2)}) collective-permute-start(bf16[24,7168]{1,0:T(8,128)(2,1)S(1)} %norm.1.refs_0_), channel_id=1, source_target_pairs={{0,192},{64,0},{128,64},{192,128},{1,193},{65,1},{129,65},{193,129... | collective-permute-start | bytes 1032200 | tf_op jit(solution)/shard_map/ppermute | solution.py:33
  129.4 9.0 %collective-permute-start.18 = (bf16[24,7168]{1,0:T(8,128)(2,1)S(1)}, bf16[24,7168]{1,0:T(8,128)(2,1)S(1)}, u32[]{:S(2)}, u32[]{:S(2)}) collective-permute-start(bf16[24,7168]{1,0:T(8,128)(2,1)S(1)} %norm.1.refs_0_), channel_id=1, source_target_pairs={{0,64},{64,128},{128,192},{192,0},{1,65},{65,129},{129,193},{193,1... | collective-permute-start | bytes 1032200 | tf_op jit(solution)/shard_map/ppermute | solution.py:33
  130.3 14.9 %collective-permute-start.22 = (bf16[24,7168]{1,0:T(8,128)(2,1)S(1)}, bf16[24,7168]{1,0:T(8,128)(2,1)S(1)}, u32[]{:S(2)}, u32[]{:S(2)}) collective-permute-start(bf16[24,7168]{1,0:T(8,128)(2,1)S(1)} %norm.1.refs_0_), channel_id=1, source_target_pairs={{0,32},{32,0},{1,33},{33,1},{2,34},{34,2},{3,35},{35,3},{4,36},{36... | collective-permute-start | bytes 1032200 | tf_op jit(solution)/shard_map/ppermute | solution.py:33
  138.5 6.7 %collective-permute-start.19 = (bf16[24,3584]{1,0:T(8,128)(2,1)S(1)}, bf16[24,3584]{1,0:T(8,128)(2,1)S(1)}, u32[]{:S(2)}, u32[]{:S(2)}) collective-permute-start(bf16[24,3584]{1,0:T(8,128)(2,1)S(1)} %slice.57), channel_id=1, source_target_pairs={{0,64},{64,128},{128,192},{192,0},{1,65},{65,129},{129,193},{193,1... | collective-permute-start | bytes 516104 | tf_op jit(solution)/shard_map/ppermute | solution.py:33
  139.3 7.2 %collective-permute-start.23 = (bf16[24,7168]{1,0:T(8,128)(2,1)S(1)}, bf16[24,7168]{1,0:T(8,128)(2,1)S(1)}, u32[]{:S(2)}, u32[]{:S(2)}) collective-permute-start(bf16[24,7168]{1,0:T(8,128)(2,1)S(1)} %collective-permute-done.18.refs_1_), channel_id=1, source_target_pairs={{0,32},{32,0},{1,33},{33,1},{2,34},{34,2},{3,35},{35,3},{4,36},{36... | collective-permute-start | bytes 1032200 | tf_op jit(solution)/shard_map/ppermute | solution.py:33
  151.8 13.6 %collective-permute-start.27 = (bf16[24,7168]{1,0:T(8,128)(2,1)S(1)}, bf16[24,7168]{1,0:T(8,128)(2,1)S(1)}, u32[]{:S(2)}, u32[]{:S(2)}) collective-permute-start(bf16[24,7168]{1,0:T(8,128)(2,1)S(1)} %get-tuple-element.20), channel_id=1, source_target_pairs={{0,32},{32,0},{1,33},{33,1},{2,34},{34,2},{3,35},{35,3},{4,36},{36... | collective-permute-start | bytes 1032200 | tf_op jit(solution)/shard_map/ppermute | solution.py:33
  154.5 10.8 %collective-permute-start.33 = (bf16[24,3584]{1,0:T(8,128)(2,1)S(1)}, bf16[24,3584]{1,0:T(8,128)(2,1)S(1)}, u32[]{:S(2)}, u32[]{:S(2)}) collective-permute-start(bf16[24,3584]{1,0:T(8,128)(2,1)S(1)} %get-tuple-element.31), channel_id=1, source_target_pairs={{0,64},{64,128},{128,192},{192,0},{1,65},{65,129},{129,193},{193,1... | collective-permute-start | bytes 516104 | tf_op jit(solution)/shard_map/ppermute | solution.py:33
  154.5 6.9 %collective-permute-start.30 = (bf16[24,3584]{1,0:T(8,128)(2,1)S(1)}, bf16[24,3584]{1,0:T(8,128)(2,1)S(1)}, u32[]{:S(2)}, u32[]{:S(2)}) collective-permute-start(bf16[24,3584]{1,0:T(8,128)(2,1)S(1)} %get-tuple-element.32), channel_id=1, source_target_pairs={{0,192},{64,0},{128,64},{192,128},{1,193},{65,1},{129,65},{193,129... | collective-permute-start | bytes 516104 | tf_op jit(solution)/shard_map/ppermute | solution.py:33
  161.5 10.2 %collective-permute-start.31 = (bf16[24,7168]{1,0:T(8,128)(2,1)S(1)}, bf16[24,7168]{1,0:T(8,128)(2,1)S(1)}, u32[]{:S(2)}, u32[]{:S(2)}) collective-permute-start(bf16[24,7168]{1,0:T(8,128)(2,1)S(1)} %pad_maximum_fusion), channel_id=1, source_target_pairs={{0,192},{64,0},{128,64},{192,128},{1,193},{65,1},{129,65},{193,129... | collective-permute-start | bytes 1032200 | tf_op jit(solution)/shard_map/ppermute | solution.py:33
  165.3 10.0 %collective-permute-start.34 = (bf16[24,7168]{1,0:T(8,128)(2,1)S(1)}, bf16[24,7168]{1,0:T(8,128)(2,1)S(1)}, u32[]{:S(2)}, u32[]{:S(2)}) collective-permute-start(bf16[24,7168]{1,0:T(8,128)(2,1)S(1)} %pad_maximum_fusion.1), channel_id=1, source_target_pairs={{0,64},{64,128},{128,192},{192,0},{1,65},{65,129},{129,193},{193,1... | collective-permute-start | bytes 1032200 | tf_op jit(solution)/shard_map/ppermute | solution.py:33
  (23 other events, 265.8 us)

commit v2 on v1

--- a/solution.py
+++ b/solution.py
@@ -20,8 +20,8 @@
 VMEM_BYTES = 48 * 1024 * 1024
 
 
-def params():
-    return pltpu.CompilerParams(vmem_limit_bytes=VMEM_BYTES)
+def params(limit=VMEM_BYTES):
+    return pltpu.CompilerParams(vmem_limit_bytes=limit)
 
 
 def whole(memory=pltpu.VMEM):
@@ -95,10 +95,10 @@
     return pl.pallas_call(
         pack_kernel,
         out_shape=jax.ShapeDtypeStruct((n_expert, span, cache.shape[2]), cache.dtype),
-        in_specs=[whole(pltpu.SMEM)] * 3 + [whole(pl.ANY)],
+        in_specs=[whole(pltpu.SMEM)] * 3 + [whole(pltpu.HBM)],
         out_specs=whole(pl.ANY),
         scratch_shapes=[pltpu.SemaphoreType.DMA((cache.shape[0],))],
-        compiler_params=params(),
+        compiler_params=params(60 * 1024 * 1024),
         name="pack_cache",
     )(owners, turns, at, cache)
 
@@ -127,10 +127,8 @@
     )(sources, arrived)
 
 
-def new_attention_kernel(lens, at, q_ref, up_ref, res_ref, *refs):
-    pieces, out_ref, latents = refs[:-2], refs[-2], refs[-1]
-    ring = len(pieces) // 2
-    pairs, span = pieces[0].shape[0], pieces[0].shape[1]
+def new_attention_kernel(lens, at, q_ref, up_ref, res_ref, near_ref, far_ref, out_ref, latents):
+    ring, pairs, span = near_ref.shape[:3]
     old = res_ref.shape[0]
     count = pairs * MOST
     heads, latent_width, value_width = up_ref.shape
@@ -142,7 +140,7 @@
         k, turn = i // MOST, i % MOST
         ours = core == turn
         cache = jnp.concatenate(
-            [jnp.where(ours, pieces[d][k], pieces[ring + d][k]) for d in range(ring)], axis=0
+            [jnp.where(ours, near_ref[d, k], far_ref[d, k]) for d in range(ring)], axis=0
         )
         scores = (
             lax.dot_general(q_ref[old + i], cache, (((1,), (1,)), ((), ())), preferred_element_type=F32)
@@ -160,18 +158,18 @@
         out_ref[:, h * value_width : (h + 1) * value_width] = rows
 
 
-def new_attention(lens, at, queries, value_up, resident, pieces):
+def new_attention(lens, at, queries, value_up, resident, near, far):
     heads, latent_width, value_width = value_up.shape
     rows = queries.shape[0]
     return pl.pallas_call(
         new_attention_kernel,
         out_shape=jax.ShapeDtypeStruct((rows, heads * value_width), BF),
-        in_specs=[whole(pltpu.SMEM)] * 2 + [whole()] * (3 + len(pieces)),
+        in_specs=[whole(pltpu.SMEM)] * 2 + [whole()] * 5,
         out_specs=whole(),
         scratch_shapes=[pltpu.VMEM((heads, rows, latent_width), F32)],
         compiler_params=params(),
         name="new_attention",
-    )(lens, at, queries, value_up, resident, *pieces)
+    )(lens, at, queries, value_up, resident, near, far)
 
 
 def stack_kernel(*refs):
@@ -189,6 +187,22 @@
         out_specs=whole(),
         compiler_params=params(),
         name="stack",
+    )(*pieces)
+
+
+def layers_kernel(*refs):
+    for k, ref in enumerate(refs[:-1]):
+        refs[-1][k] = ref[...]
+
+
+def layers(pieces):
+    return pl.pallas_call(
+        layers_kernel,
+        out_shape=jax.ShapeDtypeStruct((len(pieces),) + pieces[0].shape, pieces[0].dtype),
+        in_specs=[whole()] * len(pieces),
+        out_specs=whole(),
+        compiler_params=params(),
+        name="layers",
     )(*pieces)
 
 
@@ -210,6 +224,23 @@
         compiler_params=params(),
         name="project",
     )(makers, w_output_t, *pieces)
+
+
+def pair_kernel(a_ref, b_ref, *outs):
+    for d, out in enumerate(outs):
+        out[...] = (a_ref[d].astype(F32) + b_ref[d].astype(F32)).astype(out.dtype)
+
+
+def pair_sum(a, b):
+    out = jax.ShapeDtypeStruct(a.shape[1:], BF)
+    return pl.pallas_call(
+        pair_kernel,
+        out_shape=(out,) * a.shape[0],
+        in_specs=[whole()] * 2,
+        out_specs=(whole(),) * a.shape[0],
+        compiler_params=params(),
+        name="pair_sum",
+    )(a, b)
 
 
 def plan_kernel(rows_dev, ids_ref, gates_ref, sel_ref, mix_ref):
@@ -306,10 +337,9 @@
     )(x, gain)
 
 
-def experts_kernel(layout, *refs):
+def units_kernel(layout, *refs):
     count = sum(layout)
-    x_refs, (gate_ref, up_ref, down_ref), outs = refs[:count], refs[count : count + 3], refs[count + 3 :]
-    slots = x_refs[0].shape[0]
+    x_refs, (gate_ref, up_ref, act_ref) = refs[:count], refs[count:]
     blocks, at = [], 0
     for parts in layout:
         blocks.append(jnp.concatenate([x_refs[at + p][...] for p in range(parts)], axis=1))
@@ -317,40 +347,74 @@
     x = jnp.concatenate(blocks, axis=0)
     gate = jnp.dot(x, gate_ref[...], preferred_element_type=F32)
     up = jnp.dot(x, up_ref[...], preferred_element_type=F32)
-    act = (gate * jax.nn.sigmoid(gate) * up).astype(BF)
-    y = jnp.dot(act, down_ref[...], preferred_element_type=F32)
+    act_ref[...] = (gate * jax.nn.sigmoid(gate) * up).astype(BF)
+
+
+def run_units(layout, pieces, w_gate, w_up):
+    slots = pieces[0].shape[0] * len(layout)
+    return pl.pallas_call(
+        functools.partial(units_kernel, layout),
+        out_shape=jax.ShapeDtypeStruct((slots, w_gate.shape[1]), BF),
+        in_specs=[whole()] * (len(pieces) + 2),
+        out_specs=whole(),
+        compiler_params=params(),
+        name="units",
+    )(*pieces, w_gate, w_up)
+
+
+def down_kernel(*refs):
+    ring = len(refs) // 2 - 1
+    acts, downs, outs = refs[:ring], refs[ring : 2 * ring], refs[2 * ring :]
+    slots = acts[0].shape[0] // (2 * ring)
+    turned = []
+    for d in range(ring):
+        act = acts[d][...].astype(F32)
+        order = [core * ring + (t + ring - d) % ring for core in range(2) for t in range(ring)]
+        turned.append(jnp.concatenate([act[k * slots : (k + 1) * slots] for k in order], axis=0).astype(BF))
+    units = jnp.concatenate(turned, axis=1)
+    down = jnp.concatenate([w[...] for w in downs], axis=0)
+    y = jnp.dot(units, down, preferred_element_type=F32).astype(BF)
+    half = ring * slots
     for k, out in enumerate(outs):
-        out[...] = y[k * slots : (k + 1) * slots].astype(BF)
-
-
-def run_experts(layout, pieces, w_gate, w_up, w_down):
-    out = jax.ShapeDtypeStruct(pieces[0].shape, BF)
-    return pl.pallas_call(
-        functools.partial(experts_kernel, layout),
-        out_shape=(out,) * len(layout),
-        in_specs=[whole()] * (len(pieces) + 3),
-        out_specs=(whole(),) * len(layout),
-        compiler_params=params(),
-        name="experts",
-    )(*pieces, w_gate, w_up, w_down)
-
-
-def total_kernel(kept_ref, after_ref, before_ref, out_ref):
-    width = out_ref.shape[2]
-    total = kept_ref[...] + after_ref[...].astype(F32) + before_ref[...].astype(F32)
-    for j in range(out_ref.shape[0]):
-        out_ref[j] = total[:, j * width : (j + 1) * width].astype(BF)
-
-
-def total_by_columns(kept, after, before, parts):
-    return pl.pallas_call(
-        total_kernel,
-        out_shape=jax.ShapeDtypeStruct((parts, kept.shape[0], kept.shape[1] // parts), BF),
-        in_specs=[whole()] * 3,
-        out_specs=whole(),
-        compiler_params=params(),
-        name="total",
-    )(kept, after, before)
+        for t in range(ring):
+            at = k * half + t * slots
+            out[t] = y[at : at + slots]
+
+
+def run_down(acts, downs):
+    ring = len(acts)
+    out = jax.ShapeDtypeStruct((ring, acts[0].shape[0] // (2 * ring), downs[0].shape[1]), BF)
+    return pl.pallas_call(
+        down_kernel,
+        out_shape=(out, out),
+        in_specs=[whole()] * (2 * ring),
+        out_specs=(whole(), whole()),
+        compiler_params=params(),
+        name="down",
+    )(*acts, *downs)
+
+
+def columns_kernel(at, *refs):
+    pieces, out_ref = refs[:-1], refs[-1]
+    ring = len(pieces)
+    each, width = out_ref.shape[0] // ring, out_ref.shape[2]
+    for t, piece in enumerate(pieces):
+        first = lax.rem(at[0] + t, ring) * each
+        values = piece[...].astype(F32)
+        for j in range(each):
+            out_ref[first + j] = values[:, j * width : (j + 1) * width].astype(BF)
+
+
+def by_columns(at, pieces, parts):
+    slots, width = pieces[0].shape
+    return pl.pallas_call(
+        columns_kernel,
+        out_shape=jax.ShapeDtypeStruct((parts, slots, width * len(pieces) // parts), BF),
+        in_specs=[whole(pltpu.SMEM)] + [whole()] * len(pieces),
+        out_specs=whole(),
+        compiler_params=params(),
+        name="by_columns",
+    )(at, *pieces)
 
 
 def combine_kernel(back_ref, mix_ref, hidden_ref, out_ref):
@@ -380,18 +444,6 @@
     near = flat(near)
     far = [shifted(p, HEAD[1], 1) for p in near]
     return tuple(layout * 2), near + far
-
-
-def sum_over_head(kept, sent, parts):
-    other = {d: shifted(sent[d], HEAD[1], 1) for d in (2, 1, 3, 0)}
-    pair = [kept[d].astype(F32) + other[d].astype(F32) for d in range(4)]
-    cut = pair[2].shape[1] // 2
-    far = pair[2].astype(BF)
-    low = shifted(far[:, :cut], HEAD[0], -1).astype(F32)
-    high = shifted(far[:, cut:], HEAD[0], 1).astype(F32)
-    before = jnp.concatenate([pair[1][:, :cut] + low, pair[1][:, cut:]], axis=1).astype(BF)
-    after = jnp.concatenate([pair[3][:, :cut], pair[3][:, cut:] + high], axis=1).astype(BF)
-    return total_by_columns(pair[0], shifted(before, HEAD[0], -1), shifted(after, HEAD[0], 1), parts)
 
 
 def per_device(
@@ -439,11 +491,16 @@
     at = jnp.stack([x, core]).astype(I32)
 
     packed = pack_cache(owners, turns, at, new_cache, new_cache.shape[1] // ring, n_expert)
-    ours = select_arrived(sources, exchange(packed, EXPERT))
-    near = [ours] + [shifted(ours, HEAD[0], d) for d in range(1, ring)]
-    pieces = near + [shifted(p, HEAD[1], 1) for p in near]
+    packed, w_d = lax.optimization_barrier((packed, w_down.reshape(w_down.shape[1:])))
+    part = w_d.shape[1] // ring
+    some = lambda d: lax.dynamic_slice_in_dim(w_d, ((x + d) % ring) * part, part, 1)
+    downs = [some(0)] + [shifted(some(d), HEAD[0], d) for d in range(1, ring)]
     resident = attend(queries[:req_count], jnp.swapaxes(resident_cache, 1, 2), resident_len, value_up)
-    attention = new_attention(lens, at, queries, value_up, resident, pieces)
+    arrived, resident, *downs = lax.optimization_barrier((exchange(packed, EXPERT), resident, *downs))
+
+    ours = select_arrived(sources, arrived)
+    near = layers([ours] + [shifted(ours, HEAD[0], d) for d in range(1, ring)])
+    attention = new_attention(lens, at, queries, value_up, resident, near, shifted(near, HEAD[1], 1))
 
     along_y = [attention] + [shifted(attention, EXPERT[1], d) for d in range(1, n_y)]
     rows_here = flat(ring_gather(stacked(along_y), EXPERT[0], 0))
@@ -458,9 +515,12 @@
     received = exchange(outgoing, EXPERT)
     normed = normed_rows(received, norm_gain.reshape(1, -1))
     layout, pieces = gather_over_head(normed)
-    made = run_experts(layout, pieces, *(w.reshape(w.shape[1:]) for w in (w_gate, w_up, w_down)))
-    summed = sum_over_head(made[:ring], made[ring:], n_expert)
-    back = exchange(summed, EXPERT)
+    act = run_units(layout, pieces, w_gate.reshape(w_gate.shape[1:]), w_up.reshape(w_up.shape[1:]))
+    acts = [act] + [shifted(act, HEAD[0], d) for d in range(1, ring)]
+    kept, sent = run_down(acts, downs)
+    made = pair_sum(kept, shifted(sent, HEAD[1], 1))
+    made = list(made[:1]) + [shifted(made[t], HEAD[0], -t) for t in range(1, ring)]
+    back = exchange(by_columns(at, made, n_expert), EXPERT)
     return combine(back, mix, hidden)
 
 

time: 196 us -> 207 us (1.056)
  Pallas kernels: 17.5 us -> 22.4 us
    ppermute x35 -> x34, waiting for transfers between devices: 58.1 us -> 77.1 us  [shifted(): return lax.ppermute(x, axis, [(i, (i + step) % n) for i in range(n)])]
    all_to_all x3, waiting for transfers between devices: 37.5 us -> 20.1 us  [exchange(): return lax.all_to_all(x, axes, split_axis=0, concat_axis=0, tiled=True)]
    pallas_call x1, Pallas kernels: 1.32 us -> 5.62 us  [pack_cache(): pl.pallas_call(pack_kernel, out_shape=jax.ShapeDtypeStruct((n_expert, spa...]
    ppermute x35 -> x34, starting transfers between devices: 29.5 us -> 30.2 us  [shifted(): return lax.ppermute(x, axis, [(i, (i + step) % n) for i in range(n)])]
    pallas_call x2 -> x5, Pallas kernels: 5.2 us -> 5.79 us  [the longest x1 3.11 us: run_units(): pl.pallas_call(functools.partial(units_kernel, layout), out_shape=jax.Sha...]
  transfers between devices with their start and end apart: 38 -> 37, of which waited for: 25 -> 31; matrix products, arithmetic and copies ran while one was open for 3% -> 4% of each run, Pallas kernels for 0% -> 0%
where the time goes in v2:
time: 207 us; the launch traced here: 206 us
  waiting for transfers between devices  97.2 us (47%)
  starting transfers between devices  53.5 us (26%)
  Pallas kernels  22.4 us (11%)
  blocking collectives  20.3 us (10%)
  local copies, waits for them, and re-layouts  5.3 us (3%)
  matrix products  5.09 us (2%)
    ppermute x34, waiting for transfers between devices, shifted(): return lax.ppermute(x, axis, [(i, (i + step) % n) for i in range(n)])  77.1 us
    ppermute x34, starting transfers between devices, shifted(): return lax.ppermute(x, axis, [(i, (i + step) % n) for i in range(n)])  30.2 us
    all_to_all x3, starting transfers between devices, exchange(): return lax.all_to_all(x, axes, split_axis=0, concat_axis=0, tiled=True)  23.2 us
    all_to_all x1, blocking collectives, exchange(): return lax.all_to_all(x, axes, split_axis=0, concat_axis=0, tiled=True)  20.3 us
    all_to_all x3, waiting for transfers between devices, exchange(): return lax.all_to_all(x, axes, split_axis=0, concat_axis=0, tiled=True)  20.1 us
    pallas_call x1, Pallas kernels, pack_cache(): pl.pallas_call(pack_kernel, out_shape=jax.ShapeDtypeStruct((n_expert, spa...  5.62 us
    pallas_call x1, Pallas kernels, new_attention(): pl.pallas_call(new_attention_kernel, out_shape=jax.ShapeDtypeStruct((rows...  5.18 us
  transfers between devices with their start and end apart: 37, of which 31 were waited for; matrix products, arithmetic and copies ran while one was open for 4% of the time, Pallas kernels for 0%

profile of v2, /device:TPU:32, one launch (start us, length us, event | category | flops | bytes accessed | tf_op | source)
XLA Modules:
  0.0 206.1 jit_solution(199133772236210591)
XLA Ops:
  2.3 5.6 %pack_cache.1 = bf16[32,16,576]{2,1,0:T(8,128)(2,1)} custom-call(s32[12]{0:T(128)} %copy-done.11, s32[12]{0:T(128)} %convert_reduce_fusion.1.turns, s32[2]{0:T(128)} %pad_add_fusion.at, bf16[12,64,576]{2,1,0:T(8,128)(2,1)} %cache_ref.1), custom_call_target="tpu_custom_call" | custom-call | tf_op jit(solution)/shard_map/pack_cache/pallas_call | solution.py:95
  8.0 11.4 %all-to-all-start = ((bf16[32,16,576]{2,1,0:T(8,128)(2,1)}), bf16[32,16,576]{2,1,0:T(8,128)(2,1)S(1)}, u32[]{:S(2)}, u32[]{:S(2)}) async-start(bf16[32,16,576]{2,1,0:T(8,128)(2,1)} %pack_cache.1), calls=%async_computation | async-start | bytes 1310720 | tf_op jit(solution)/shard_map/all_to_all | solution.py:438
  20.6 2.8 %collective-permute-start.2 = (bf16[128,1792]{1,0:T(8,128)(2,1)}, bf16[128,1792]{1,0:T(8,128)(2,1)}, u32[]{:S(2)}, u32[]{:S(2)}) collective-permute-start(bf16[128,1792]{1,0:T(8,128)(2,1)} %get-tuple-element.43), channel_id=1, source_target_pairs={{0,192},{64,0},{128,64},{192,128},{1,193},{65,1},{129,65},{193,129... | collective-permute-start | bytes 1376264 | tf_op jit(solution)/shard_map/ppermute | solution.py:33
  30.8 12.0 %collective-permute-done.2.refs_7_ = bf16[128,1792]{1,0:T(8,128)(2,1)} collective-permute-done((bf16[128,1792]{1,0:T(8,128)(2,1)}, bf16[128,1792]{1,0:T(8,128)(2,1)}, u32[]{:S(2)}, u32[]{:S(2)}) %collective-permute-start.2) | collective-permute-done | bytes 458784 | tf_op jit(solution)/shard_map/ppermute | solution.py:33
  42.8 3.7 %collective-permute-done.refs_5_ = bf16[128,1792]{1,0:T(8,128)(2,1)} collective-permute-done((bf16[128,1792]{1,0:T(8,128)(2,1)}, bf16[128,1792]{1,0:T(8,128)(2,1)}, u32[]{:S(2)}, u32[]{:S(2)}) %collective-permute-start) | collective-permute-done | bytes 458784 | tf_op jit(solution)/shard_map/ppermute | solution.py:33
  49.5 4.0 %collective-permute-done.5.refs_3_ = bf16[6,16,576]{2,1,0:T(8,128)(2,1)S(1)} collective-permute-done((bf16[6,16,576]{2,1,0:T(8,128)(2,1)S(1)}, bf16[6,16,576]{2,1,0:T(8,128)(2,1)S(1)}, u32[]{:S(2)}, u32[]{:S(2)}) %collective-permute-start.5) | collective-permute-done | bytes 110624 | tf_op jit(solution)/shard_map/ppermute | solution.py:33
  58.8 5.2 %new_attention.1.refs_0_ = bf16[16,2048]{1,0:T(8,128)(2,1)S(1)} custom-call(s32[12]{0:T(128)S(1)} %get-tuple-element.42.lens, s32[2]{0:T(128)S(1)} %copy-done.5, bf16[16,16,576]{2,1,0:T(8,128)(2,1)S(1)} %copy-done.3, bf16[16,512,128]{2,1,0:T(8,128)(2,1)S(1)} %copy-done.1, bf16[4,2048]{1,0:T(4,128)(2,1)S(1)} %fusion.4.res_ref, ...), custom_call_target="tpu_custom_call" | custom-call | tf_op jit(solution)/shard_map/new_attention/pallas_call | solution.py:164
  64.0 2.8 %collective-permute-start.9 = (bf16[16,2048]{1,0:T(8,128)(2,1)S(1)}, bf16[16,2048]{1,0:T(8,128)(2,1)S(1)}, u32[]{:S(2)}, u32[]{:S(2)}) collective-permute-start(bf16[16,2048]{1,0:T(8,128)(2,1)S(1)} %new_attention.1.refs_0_), channel_id=1, source_target_pairs={{0,3},{1,0},{2,1},{3,2},{4,7},{5,4},{6,5},{7,6},{8,11},{9,8},{10,9... | collective-permute-start | bytes 196616 | tf_op jit(solution)/shard_map/ppermute | solution.py:33
  69.9 2.9 %collective-permute-done.8.refs_2_ = bf16[16,2048]{1,0:T(8,128)(2,1)S(1)} collective-permute-done((bf16[16,2048]{1,0:T(8,128)(2,1)S(1)}, bf16[16,2048]{1,0:T(8,128)(2,1)S(1)}, u32[]{:S(2)}, u32[]{:S(2)}) %collective-permute-start.8) | collective-permute-done | bytes 65568 | tf_op jit(solution)/shard_map/ppermute | solution.py:33
  75.6 5.2 %collective-permute-done.14.refs_8_ = bf16[64,2048]{1,0:T(8,128)(2,1)S(1)} collective-permute-done((bf16[64,2048]{1,0:T(8,128)(2,1)S(1)}, bf16[64,2048]{1,0:T(8,128)(2,1)S(1)}, u32[]{:S(2)}, u32[]{:S(2)}) %collective-permute-start.14) | collective-permute-done | bytes 262176 | tf_op jit(solution)/shard_map/ppermute | solution.py:33
  82.8 4.3 %collective-permute-done.15.refs_7_ = bf16[64,2048]{1,0:T(8,128)(2,1)S(1)} collective-permute-done((bf16[64,2048]{1,0:T(8,128)(2,1)S(1)}, bf16[64,2048]{1,0:T(8,128)(2,1)S(1)}, u32[]{:S(2)}, u32[]{:S(2)}) %collective-permute-start.15) | collective-permute-done | bytes 262176 | tf_op jit(solution)/shard_map/ppermute | solution.py:33
  89.7 4.1 %collective-permute-done.16.refs_6_ = bf16[64,2048]{1,0:T(8,128)(2,1)S(1)} collective-permute-done((bf16[64,2048]{1,0:T(8,128)(2,1)S(1)}, bf16[64,2048]{1,0:T(8,128)(2,1)S(1)}, u32[]{:S(2)}, u32[]{:S(2)}) %collective-permute-start.16) | collective-permute-done | bytes 262176 | tf_op jit(solution)/shard_map/ppermute | solution.py:33
  93.8 3.3 %collective-permute-start.17 = (bf16[32,2048]{1,0:T(8,128)(2,1)S(1)}, bf16[32,2048]{1,0:T(8,128)(2,1)S(1)}, u32[]{:S(2)}, u32[]{:S(2)}) collective-permute-start(bf16[32,2048]{1,0:T(8,128)(2,1)S(1)} %slice.30), channel_id=1, source_target_pairs={{0,28},{4,0},{8,4},{12,8},{16,12},{20,16},{24,20},{28,24},{1,29},{... | collective-permute-start | bytes 393224 | tf_op jit(solution)/shard_map/ppermute | solution.py:33
  99.9 4.1 %collective-permute-done.13.refs_4_ = bf16[32,2048]{1,0:T(8,128)(2,1)S(1)} collective-permute-done((bf16[32,2048]{1,0:T(8,128)(2,1)S(1)}, bf16[32,2048]{1,0:T(8,128)(2,1)S(1)}, u32[]{:S(2)}, u32[]{:S(2)}) %collective-permute-start.13) | collective-permute-done | bytes 131104 | tf_op jit(solution)/shard_map/ppermute | solution.py:33
  107.1 3.5 %all-to-all-start.1 = ((bf16[8,64,224]{2,1,0:T(8,128)(2,1)}), bf16[8,64,224]{2,1,0:T(8,128)(2,1)S(1)}, u32[]{:S(2)}, u32[]{:S(2)}) async-start(bf16[8,64,224]{2,1,0:T(8,128)(2,1)} %bitcast.7), calls=%async_computation.1 | async-start | bytes 524288 | tf_op jit(solution)/shard_map/all_to_all | solution.py:438
  112.3 5.8 %all-to-all-done.1.parts_ref = bf16[8,64,224]{2,1,0:T(8,128)(2,1)S(1)} async-done(((bf16[8,64,224]{2,1,0:T(8,128)(2,1)}), bf16[8,64,224]{2,1,0:T(8,128)(2,1)S(1)}, u32[]{:S(2)}, u32[]{:S(2)}) %all-to-all-start.1) | async-done | bytes 229408 | tf_op jit(solution)/shard_map/all_to_all | solution.py:438
  119.2 8.3 %all-to-all-start.2 = ((bf16[32,24,224]{2,1,0:T(8,128)(2,1)}), bf16[32,24,224]{2,1,0:T(8,128)(2,1)S(1)}, u32[]{:S(2)}, u32[]{:S(2)}) async-start(bf16[32,24,224]{2,1,0:T(8,128)(2,1)} %get-tuple-element.28), calls=%async_computation.2 | async-start | bytes 786432 | tf_op jit(solution)/shard_map/all_to_all | solution.py:438
  127.6 14.3 %all-to-all-done.2.x_ref = bf16[32,24,224]{2,1,0:T(8,128)(2,1)S(1)} async-done(((bf16[32,24,224]{2,1,0:T(8,128)(2,1)}), bf16[32,24,224]{2,1,0:T(8,128)(2,1)S(1)}, u32[]{:S(2)}, u32[]{:S(2)}) %all-to-all-start.2) | async-done | bytes 344096 | tf_op jit(solution)/shard_map/all_to_all | solution.py:438
  144.2 6.8 %collective-permute-done.20.refs_4_ = bf16[24,7168]{1,0:T(8,128)(2,1)S(1)} collective-permute-done((bf16[24,7168]{1,0:T(8,128)(2,1)S(1)}, bf16[24,7168]{1,0:T(8,128)(2,1)S(1)}, u32[]{:S(2)}, u32[]{:S(2)}) %collective-permute-start.20) | collective-permute-done | bytes 344096 | tf_op jit(solution)/shard_map/ppermute | solution.py:33
  153.7 2.8 %collective-permute-done.21.refs_3_ = bf16[24,3584]{1,0:T(8,128)(2,1)S(1)} collective-permute-done((bf16[24,3584]{1,0:T(8,128)(2,1)S(1)}, bf16[24,3584]{1,0:T(8,128)(2,1)S(1)}, u32[]{:S(2)}, u32[]{:S(2)}) %collective-permute-start.21) | collective-permute-done | bytes 172064 | tf_op jit(solution)/shard_map/ppermute | solution.py:33
  160.5 3.1 %units.1.refs_0_ = bf16[192,128]{1,0:T(8,128)(2,1)S(1)} custom-call(bf16[24,7168]{1,0:T(8,128)(2,1)S(1)} %norm.1.refs_0_, bf16[24,7168]{1,0:T(8,128)(2,1)S(1)} %collective-permute-done.18.refs_1_, bf16[24,3584]{1,0:T(8,128)(2,1)S(1)} %collective-permute-done.19.refs_2_, bf16[24,3584]{1,0:T(8,128)(2,1)S(1)} %collective-permute-done.21.refs_3_, ...), custom_call_target="tpu_custom_call" | custom-call | tf_op jit(solution)/shard_map/units/pallas_call | solution.py:355
  177.2 3.0 %collective-permute-done.31.refs_1_ = bf16[24,1792]{1,0:T(8,128)(2,1)S(1)} collective-permute-done((bf16[24,1792]{1,0:T(8,128)(2,1)S(1)}, bf16[24,1792]{1,0:T(8,128)(2,1)S(1)}, u32[]{:S(2)}, u32[]{:S(2)}) %collective-permute-start.31) | collective-permute-done | bytes 86048 | tf_op jit(solution)/shard_map/ppermute | solution.py:33
  180.2 2.8 %collective-permute-done.32.refs_2_ = bf16[24,1792]{1,0:T(8,128)(2,1)S(1)} collective-permute-done((bf16[24,1792]{1,0:T(8,128)(2,1)S(1)}, bf16[24,1792]{1,0:T(8,128)(2,1)S(1)}, u32[]{:S(2)}, u32[]{:S(2)}) %collective-permute-start.32) | collective-permute-done | bytes 86048 | tf_op jit(solution)/shard_map/ppermute | solution.py:33
  184.6 20.3 %all_to_all.20.back_ref = bf16[32,24,224]{2,1,0:T(8,128)(2,1)S(1)} all-to-all(bf16[32,24,224]{2,1,0:T(8,128)(2,1)S(1)} %by_columns.1), channel_id=1, replica_groups=mesh['head_0'=4,'head_1'=2,'expert_0'=8,'expert_1'=4] {'expert_0','exper..., dimensions={0} | all-to-all | bytes 688128 | tf_op jit(solution)/shard_map/all_to_all | solution.py:438
  (114 shorter events, 63.7 us)
Async XLA Ops:
  8.0 38.5 %all-to-all-start = ((bf16[32,16,576]{2,1,0:T(8,128)(2,1)}), bf16[32,16,576]{2,1,0:T(8,128)(2,1)S(1)}, u32[]{:S(2)}, u32[]{:S(2)}) async-start(bf16[32,16,576]{2,1,0:T(8,128)(2,1)} %pack_cache.1), calls=%async_computation | async-start | bytes 1310720 | tf_op jit(solution)/shard_map/all_to_all | solution.py:438
  20.6 22.2 %collective-permute-start.2 = (bf16[128,1792]{1,0:T(8,128)(2,1)}, bf16[128,1792]{1,0:T(8,128)(2,1)}, u32[]{:S(2)}, u32[]{:S(2)}) collective-permute-start(bf16[128,1792]{1,0:T(8,128)(2,1)} %get-tuple-element.43), channel_id=1, source_target_pairs={{0,192},{64,0},{128,64},{192,128},{1,193},{65,1},{129,65},{193,129... | collective-permute-start | bytes 1376264 | tf_op jit(solution)/shard_map/ppermute | solution.py:33
  23.3 19.4 %collective-permute-start.1 = (bf16[128,1792]{1,0:T(8,128)(2,1)}, bf16[128,1792]{1,0:T(8,128)(2,1)}, u32[]{:S(2)}, u32[]{:S(2)}) collective-permute-start(bf16[128,1792]{1,0:T(8,128)(2,1)} %get-tuple-element.44), channel_id=1, source_target_pairs={{0,128},{64,192},{128,0},{192,64},{1,129},{65,193},{129,1},{193,65... | collective-permute-start | bytes 1376264 | tf_op jit(solution)/shard_map/ppermute | solution.py:33
  24.1 22.3 %collective-permute-start = (bf16[128,1792]{1,0:T(8,128)(2,1)}, bf16[128,1792]{1,0:T(8,128)(2,1)}, u32[]{:S(2)}, u32[]{:S(2)}) collective-permute-start(bf16[128,1792]{1,0:T(8,128)(2,1)} %get-tuple-element.45), channel_id=1, source_target_pairs={{0,64},{64,128},{128,192},{192,0},{1,65},{65,129},{129,193},{193,1... | collective-permute-start | bytes 1376264 | tf_op jit(solution)/shard_map/ppermute | solution.py:33
  47.2 6.3 %collective-permute-start.5 = (bf16[6,16,576]{2,1,0:T(8,128)(2,1)S(1)}, bf16[6,16,576]{2,1,0:T(8,128)(2,1)S(1)}, u32[]{:S(2)}, u32[]{:S(2)}) collective-permute-start(bf16[6,16,576]{2,1,0:T(8,128)(2,1)S(1)} %select_arrived.1.refs_0_), channel_id=1, source_target_pairs={{0,192},{64,0},{128,64},{192,128},{1,193},{65,1},{129,65},{193,129... | collective-permute-start | bytes 331784 | tf_op jit(solution)/shard_map/ppermute | solution.py:33
  47.9 7.3 %collective-permute-start.4 = (bf16[6,16,576]{2,1,0:T(8,128)(2,1)S(1)}, bf16[6,16,576]{2,1,0:T(8,128)(2,1)S(1)}, u32[]{:S(2)}, u32[]{:S(2)}) collective-permute-start(bf16[6,16,576]{2,1,0:T(8,128)(2,1)S(1)} %select_arrived.1.refs_0_), channel_id=1, source_target_pairs={{0,128},{64,192},{128,0},{192,64},{1,129},{65,193},{129,1},{193,65... | collective-permute-start | bytes 331784 | tf_op jit(solution)/shard_map/ppermute | solution.py:33
  48.7 8.1 %collective-permute-start.3 = (bf16[6,16,576]{2,1,0:T(8,128)(2,1)S(1)}, bf16[6,16,576]{2,1,0:T(8,128)(2,1)S(1)}, u32[]{:S(2)}, u32[]{:S(2)}) collective-permute-start(bf16[6,16,576]{2,1,0:T(8,128)(2,1)S(1)} %select_arrived.1.refs_0_), channel_id=1, source_target_pairs={{0,64},{64,128},{128,192},{192,0},{1,65},{65,129},{129,193},{193,1... | collective-permute-start | bytes 331784 | tf_op jit(solution)/shard_map/ppermute | solution.py:33
  66.7 6.1 %collective-permute-start.8 = (bf16[16,2048]{1,0:T(8,128)(2,1)S(1)}, bf16[16,2048]{1,0:T(8,128)(2,1)S(1)}, u32[]{:S(2)}, u32[]{:S(2)}) collective-permute-start(bf16[16,2048]{1,0:T(8,128)(2,1)S(1)} %new_attention.1.refs_0_), channel_id=1, source_target_pairs={{0,2},{1,3},{2,0},{3,1},{4,6},{5,7},{6,4},{7,5},{8,10},{9,11},{10,... | collective-permute-start | bytes 196616 | tf_op jit(solution)/shard_map/ppermute | solution.py:33
  73.5 7.3 %collective-permute-start.14 = (bf16[64,2048]{1,0:T(8,128)(2,1)S(1)}, bf16[64,2048]{1,0:T(8,128)(2,1)S(1)}, u32[]{:S(2)}, u32[]{:S(2)}) collective-permute-start(bf16[64,2048]{1,0:T(8,128)(2,1)S(1)} %stack.13.refs_0_), channel_id=1, source_target_pairs={{0,28},{4,0},{8,4},{12,8},{16,12},{20,16},{24,20},{28,24},{1,29},{... | collective-permute-start | bytes 786440 | tf_op jit(solution)/shard_map/ppermute | solution.py:33
  74.1 7.9 %collective-permute-start.10 = (bf16[64,2048]{1,0:T(8,128)(2,1)S(1)}, bf16[64,2048]{1,0:T(8,128)(2,1)S(1)}, u32[]{:S(2)}, u32[]{:S(2)}) collective-permute-start(bf16[64,2048]{1,0:T(8,128)(2,1)S(1)} %stack.13.refs_0_), channel_id=1, source_target_pairs={{0,4},{4,8},{8,12},{12,16},{16,20},{20,24},{24,28},{28,0},{1,5},{5... | collective-permute-start | bytes 786440 | tf_op jit(solution)/shard_map/ppermute | solution.py:33
  80.8 6.4 %collective-permute-start.15 = (bf16[64,2048]{1,0:T(8,128)(2,1)S(1)}, bf16[64,2048]{1,0:T(8,128)(2,1)S(1)}, u32[]{:S(2)}, u32[]{:S(2)}) collective-permute-start(bf16[64,2048]{1,0:T(8,128)(2,1)S(1)} %collective-permute-done.14.refs_8_), channel_id=1, source_target_pairs={{0,28},{4,0},{8,4},{12,8},{16,12},{20,16},{24,20},{28,24},{1,29},{... | collective-permute-start | bytes 786440 | tf_op jit(solution)/shard_map/ppermute | solution.py:33
  82.1 7.6 %collective-permute-start.11 = (bf16[64,2048]{1,0:T(8,128)(2,1)S(1)}, bf16[64,2048]{1,0:T(8,128)(2,1)S(1)}, u32[]{:S(2)}, u32[]{:S(2)}) collective-permute-start(bf16[64,2048]{1,0:T(8,128)(2,1)S(1)} %collective-permute-done.10.refs_1_), channel_id=1, source_target_pairs={{0,4},{4,8},{8,12},{12,16},{16,20},{20,24},{24,28},{28,0},{1,5},{5... | collective-permute-start | bytes 786440 | tf_op jit(solution)/shard_map/ppermute | solution.py:33
  87.1 6.6 %collective-permute-start.16 = (bf16[64,2048]{1,0:T(8,128)(2,1)S(1)}, bf16[64,2048]{1,0:T(8,128)(2,1)S(1)}, u32[]{:S(2)}, u32[]{:S(2)}) collective-permute-start(bf16[64,2048]{1,0:T(8,128)(2,1)S(1)} %collective-permute-done.15.refs_7_), channel_id=1, source_target_pairs={{0,28},{4,0},{8,4},{12,8},{16,12},{20,16},{24,20},{28,24},{1,29},{... | collective-permute-start | bytes 786440 | tf_op jit(solution)/shard_map/ppermute | solution.py:33
  89.7 7.8 %collective-permute-start.12 = (bf16[64,2048]{1,0:T(8,128)(2,1)S(1)}, bf16[64,2048]{1,0:T(8,128)(2,1)S(1)}, u32[]{:S(2)}, u32[]{:S(2)}) collective-permute-start(bf16[64,2048]{1,0:T(8,128)(2,1)S(1)} %collective-permute-done.11.refs_2_), channel_id=1, source_target_pairs={{0,4},{4,8},{8,12},{12,16},{16,20},{20,24},{24,28},{28,0},{1,5},{5... | collective-permute-start | bytes 786440 | tf_op jit(solution)/shard_map/ppermute | solution.py:33
  97.4 6.5 %collective-permute-start.13 = (bf16[32,2048]{1,0:T(8,128)(2,1)S(1)}, bf16[32,2048]{1,0:T(8,128)(2,1)S(1)}, u32[]{:S(2)}, u32[]{:S(2)}) collective-permute-start(bf16[32,2048]{1,0:T(8,128)(2,1)S(1)} %slice.29), channel_id=1, source_target_pairs={{0,4},{4,8},{8,12},{12,16},{16,20},{20,24},{24,28},{28,0},{1,5},{5... | collective-permute-start | bytes 393224 | tf_op jit(solution)/shard_map/ppermute | solution.py:33
  107.1 11.0 %all-to-all-start.1 = ((bf16[8,64,224]{2,1,0:T(8,128)(2,1)}), bf16[8,64,224]{2,1,0:T(8,128)(2,1)S(1)}, u32[]{:S(2)}, u32[]{:S(2)}) async-start(bf16[8,64,224]{2,1,0:T(8,128)(2,1)} %bitcast.7), calls=%async_computation.1 | async-start | bytes 524288 | tf_op jit(solution)/shard_map/all_to_all | solution.py:438
  119.2 22.7 %all-to-all-start.2 = ((bf16[32,24,224]{2,1,0:T(8,128)(2,1)}), bf16[32,24,224]{2,1,0:T(8,128)(2,1)S(1)}, u32[]{:S(2)}, u32[]{:S(2)}) async-start(bf16[32,24,224]{2,1,0:T(8,128)(2,1)} %get-tuple-element.28), calls=%async_computation.2 | async-start | bytes 786432 | tf_op jit(solution)/shard_map/all_to_all | solution.py:438
  142.1 8.9 %collective-permute-start.20 = (bf16[24,7168]{1,0:T(8,128)(2,1)S(1)}, bf16[24,7168]{1,0:T(8,128)(2,1)S(1)}, u32[]{:S(2)}, u32[]{:S(2)}) collective-permute-start(bf16[24,7168]{1,0:T(8,128)(2,1)S(1)} %norm.1.refs_0_), channel_id=1, source_target_pairs={{0,192},{64,0},{128,64},{192,128},{1,193},{65,1},{129,65},{193,129... | collective-permute-start | bytes 1032200 | tf_op jit(solution)/shard_map/ppermute | solution.py:33
  143.3 9.0 %collective-permute-start.18 = (bf16[24,7168]{1,0:T(8,128)(2,1)S(1)}, bf16[24,7168]{1,0:T(8,128)(2,1)S(1)}, u32[]{:S(2)}, u32[]{:S(2)}) collective-permute-start(bf16[24,7168]{1,0:T(8,128)(2,1)S(1)} %norm.1.refs_0_), channel_id=1, source_target_pairs={{0,64},{64,128},{128,192},{192,0},{1,65},{65,129},{129,193},{193,1... | collective-permute-start | bytes 1032200 | tf_op jit(solution)/shard_map/ppermute | solution.py:33
  144.2 14.9 %collective-permute-start.22 = (bf16[24,7168]{1,0:T(8,128)(2,1)S(1)}, bf16[24,7168]{1,0:T(8,128)(2,1)S(1)}, u32[]{:S(2)}, u32[]{:S(2)}) collective-permute-start(bf16[24,7168]{1,0:T(8,128)(2,1)S(1)} %norm.1.refs_0_), channel_id=1, source_target_pairs={{0,32},{32,0},{1,33},{33,1},{2,34},{34,2},{3,35},{35,3},{4,36},{36... | collective-permute-start | bytes 1032200 | tf_op jit(solution)/shard_map/ppermute | solution.py:33
  152.4 6.7 %collective-permute-start.19 = (bf16[24,3584]{1,0:T(8,128)(2,1)S(1)}, bf16[24,3584]{1,0:T(8,128)(2,1)S(1)}, u32[]{:S(2)}, u32[]{:S(2)}) collective-permute-start(bf16[24,3584]{1,0:T(8,128)(2,1)S(1)} %slice.31), channel_id=1, source_target_pairs={{0,64},{64,128},{128,192},{192,0},{1,65},{65,129},{129,193},{193,1... | collective-permute-start | bytes 516104 | tf_op jit(solution)/shard_map/ppermute | solution.py:33
  153.2 7.2 %collective-permute-start.23 = (bf16[24,7168]{1,0:T(8,128)(2,1)S(1)}, bf16[24,7168]{1,0:T(8,128)(2,1)S(1)}, u32[]{:S(2)}, u32[]{:S(2)}) collective-permute-start(bf16[24,7168]{1,0:T(8,128)(2,1)S(1)} %collective-permute-done.18.refs_1_), channel_id=1, source_target_pairs={{0,32},{32,0},{1,33},{33,1},{2,34},{34,2},{3,35},{35,3},{4,36},{36... | collective-permute-start | bytes 1032200 | tf_op jit(solution)/shard_map/ppermute | solution.py:33
  176.2 6.7 %collective-permute-start.32 = (bf16[24,1792]{1,0:T(8,128)(2,1)S(1)}, bf16[24,1792]{1,0:T(8,128)(2,1)S(1)}, u32[]{:S(2)}, u32[]{:S(2)}) collective-permute-start(bf16[24,1792]{1,0:T(8,128)(2,1)S(1)} %get-tuple-element.37), channel_id=1, source_target_pairs={{0,128},{64,192},{128,0},{192,64},{1,129},{65,193},{129,1},{193,65... | collective-permute-start | bytes 258056 | tf_op jit(solution)/shard_map/ppermute | solution.py:33
  177.1 6.7 %collective-permute-start.33 = (bf16[24,1792]{1,0:T(8,128)(2,1)S(1)}, bf16[24,1792]{1,0:T(8,128)(2,1)S(1)}, u32[]{:S(2)}, u32[]{:S(2)}) collective-permute-start(bf16[24,1792]{1,0:T(8,128)(2,1)S(1)} %get-tuple-element.38), channel_id=1, source_target_pairs={{0,64},{64,128},{128,192},{192,0},{1,65},{65,129},{129,193},{193,1... | collective-permute-start | bytes 258056 | tf_op jit(solution)/shard_map/ppermute | solution.py:33
  (25 other events, 335.6 us)
